TPU v7x, 32 devices: a whole 2x2x4 slice. The times are simulated.
32 devices in a mesh: segment: 4 (over z), exp: 8 (over y, x, core).
Axes of the slice: x: 2, y: 2, z: 4, core: 2. Of those that a mesh axis runs over, the one named last changes fastest.
Arguments:
- hidden_rows: bfloat16 [4096, 2048], P(('segment', 'exp')), may hold values from -60 to 60, as said below
- norm_gain: float32 [2048], replicated, may hold values from 0.5 to 1.5
- router_weight: bfloat16 [2048, 16], replicated, may hold values from -0.25 to 0.25
- expert_ids: int32 [4096, 6], P(('segment', 'exp')), may hold values from 0 to 15, all different within a row; in each aligned block of 64 rows (0 to 63, 64 to 127, ...) at most 30 rows name the same one
- gate_weight: bfloat16 [4, 8, 704, 2048], P('segment', 'exp'), may hold values from -0.125 to 0.125
- up_weight: bfloat16 [4, 8, 704, 2048], P('segment', 'exp'), may hold values from -0.125 to 0.125
- down_weight: bfloat16 [4, 8, 704, 2048], P('segment', 'exp'), may hold values from -0.15625 to 0.15625
- latent_gain: float32 [2048], replicated, may hold values from 0.5 to 1.5
- kv_weight: bfloat16 [2048, 512], replicated, may hold values from -0.125 to 0.125
Outputs:
- expert_mix: bfloat16 [4096, 2048], P(('segment', 'exp'))
- latents: bfloat16 [4096, 512], P(('segment', 'exp'))
- gram_input: float32 [4, 8, 1024, 2048], P('segment', 'exp')
- gram_hidden: float32 [4, 8, 704, 1408], P('segment', 'exp')
Inputs may be any that keep to these rules, and one draw needn't show every extreme that they name: `expert_ids`: each row names 6 different experts and every expert is named somewhere. In each aligned block of 64 rows (one micro-batch of one device) no expert is named more than 30 times, and in some blocks some expert is named exactly 30 times. `hidden_rows`: activations of the attention section.
All inputs are finite; a program needn't handle non-finite values.
Results may differ from a plain program's by a relative error of at most 0.0068.
Values may be sent and summed in bfloat16 or wider, within the bound.
A program may use at most 192 MiB of HBM per device.

v0:
```python
import jax
import jax.numpy as jnp
from jax import lax
from jax.sharding import PartitionSpec as P

MB_TOK = 64


def swapped(value, axis, stride):
    mask = 2**stride
    pairs = [(source, source ^ mask) for source in range(lax.axis_size(axis))]
    return lax.ppermute(value, axis, pairs)


def rms_norm(values, gain):
    mean_square = jnp.mean(values * values, axis=-1, keepdims=True)
    return values * lax.rsqrt(mean_square + 1e-06) * gain


def body(
    hidden_rows,
    norm_gain,
    router_weight,
    expert_ids,
    gate_weight,
    up_weight,
    down_weight,
    latent_gain,
    kv_weight,
):
    segments = lax.axis_size("segment")
    columns = lax.axis_size("exp")
    devices = segments * columns
    pair_count = segments // 2
    model_width = hidden_rows.shape[1]
    width_half = model_width // 2
    experts = router_weight.shape[1]
    top_count = expert_ids.shape[1]
    tok_rows = hidden_rows.shape[0]
    micro_rows = MB_TOK
    capacity = micro_rows * top_count * 5 // (4 * experts)
    half_index = lax.axis_index("segment") % 2
    w_gate = gate_weight[0, 0]
    w_up = up_weight[0, 0]
    w_down = down_weight[0, 0]
    half_units = w_gate.shape[0]
    slot_rows = devices * capacity
    own_rows = lax.dynamic_slice_in_dim(w_down, half_index * width_half, width_half, 1)
    sent_rows = lax.dynamic_slice_in_dim(w_down, (1 - half_index) * width_half, width_half, 1)
    other_rows = swapped(sent_rows, "segment", 0)
    down_block = jnp.where(
        half_index == 0,
        jnp.concatenate([own_rows, other_rows], axis=0),
        jnp.concatenate([other_rows, own_rows], axis=0),
    )
    residual = hidden_rows.astype(jnp.float32)
    normed = rms_norm(residual, norm_gain).astype(jnp.bfloat16)
    logits = jnp.dot(normed, router_weight, preferred_element_type=jnp.float32)
    expert_grid = jnp.arange(experts, dtype=jnp.int32)
    choose = expert_ids[:, :, None] == expert_grid[None, None, :]
    picked = jnp.sum(jnp.where(choose, logits[:, None, :], 0.0), axis=2)
    affinity = jax.nn.sigmoid(picked)
    gate_share = affinity / jnp.sum(affinity, axis=1, keepdims=True)
    gram_in = jnp.zeros((width_half, model_width), jnp.float32)
    gram_hid = jnp.zeros((half_units, 2 * half_units), jnp.float32)
    count_total = jnp.zeros((), jnp.float32)
    mix_blocks = []
    positions = jnp.arange(experts * capacity, dtype=jnp.int32)
    for step_index in range(tok_rows // micro_rows):
        low = step_index * micro_rows
        block_rows = normed[low : low + micro_rows]
        block_ids = expert_ids[low : low + micro_rows]
        block_gates = gate_share[low : low + micro_rows]
        flat_ids = block_ids.reshape(-1)
        onehot = (flat_ids[:, None] == expert_grid[None, :]).astype(jnp.int32)
        slot_rank = jnp.sum((jnp.cumsum(onehot, axis=0) - onehot) * onehot, axis=1)
        target = (flat_ids * capacity + slot_rank).reshape(micro_rows, top_count)
        picker = target[:, :, None] == positions[None, None, :]
        dispatch_table = jnp.any(picker, axis=1).astype(jnp.bfloat16)
        combine_table = jnp.sum(jnp.where(picker, block_gates[:, :, None], 0.0), axis=1)
        buffer = lax.dot_general(
            dispatch_table, block_rows, (((0,), (0,)), ((), ())), preferred_element_type=jnp.float32
        ).astype(jnp.bfloat16)
        sent_counts = jnp.sum(onehot, axis=0).astype(jnp.bfloat16)
        grid_rows = jnp.broadcast_to(
            buffer.reshape(pair_count, 1, columns, capacity, model_width),
            (pair_count, 2, columns, capacity, model_width),
        ).reshape(devices, capacity, model_width)
        grid_counts = jnp.broadcast_to(
            sent_counts.reshape(pair_count, 1, columns), (pair_count, 2, columns)
        ).reshape(devices, 1)
        arrived, arrived_counts = (
            lax.all_to_all(grid_rows, ("segment", "exp"), split_axis=0, concat_axis=0, tiled=True),
            lax.all_to_all(
                grid_counts, ("segment", "exp"), split_axis=0, concat_axis=0, tiled=True
            ),
        )
        received = arrived.reshape(slot_rows, model_width)
        count_total = count_total + jnp.sum(arrived_counts.astype(jnp.float32))
        gate_pre = lax.dot_general(
            w_gate, received, (((1,), (1,)), ((), ())), preferred_element_type=jnp.float32
        )
        up_pre = lax.dot_general(
            w_up, received, (((1,), (1,)), ((), ())), preferred_element_type=jnp.float32
        )
        hidden_t = (jax.nn.silu(gate_pre) * up_pre).astype(jnp.bfloat16)
        own_columns = lax.dynamic_slice_in_dim(received, half_index * width_half, width_half, 1)
        gram_in = gram_in + lax.dot_general(
            own_columns, received, (((0,), (0,)), ((), ())), preferred_element_type=jnp.float32
        )
        other_hidden = swapped(hidden_t, "segment", 0)
        first_half = jnp.where(half_index == 0, hidden_t, other_hidden)
        second_half = jnp.where(half_index == 0, other_hidden, hidden_t)
        full_hidden = jnp.concatenate([first_half, second_half], axis=0)
        gram_hid = gram_hid + lax.dot_general(
            hidden_t, full_hidden, (((1,), (1,)), ((), ())), preferred_element_type=jnp.float32
        )
        column_half = lax.dot_general(
            full_hidden, down_block, (((0,), (0,)), ((), ())), preferred_element_type=jnp.float32
        )
        returned = lax.all_to_all(
            column_half.reshape(devices, capacity, width_half),
            ("segment", "exp"),
            split_axis=0,
            concat_axis=0,
            tiled=True,
        )
        expert_rows = (
            returned.reshape(pair_count, 2, columns, capacity, width_half)
            .transpose(0, 2, 3, 1, 4)
            .reshape(experts * capacity, model_width)
        )
        mix_rows = jnp.dot(
            combine_table,
            expert_rows,
            precision=lax.Precision.HIGHEST,
            preferred_element_type=jnp.float32,
        )
        mix_blocks.append(mix_rows)
    expert_mix = jnp.concatenate(mix_blocks, axis=0).astype(jnp.bfloat16)
    combined = residual + expert_mix.astype(jnp.float32)
    normed_next = rms_norm(combined, latent_gain).astype(jnp.bfloat16)
    latents = jnp.dot(normed_next, kv_weight, preferred_element_type=jnp.float32).astype(
        jnp.bfloat16
    )
    inverse_count = 2.0 / count_total
    gram_input = (gram_in * inverse_count)[None, None]
    gram_hidden = (gram_hid * inverse_count)[None, None]
    return (expert_mix, latents, gram_input, gram_hidden)


def solution(mesh):
    return jax.shard_map(
        body,
        mesh=mesh,
        in_specs=(
            P(("segment", "exp"), None),
            P(),
            P(),
            P(("segment", "exp"), None),
            P("segment", "exp", None, None),
            P("segment", "exp", None, None),
            P("segment", "exp", None, None),
            P(),
            P(),
        ),
        out_specs=(
            P(("segment", "exp"), None),
            P(("segment", "exp"), None),
            P("segment", "exp", None, None),
            P("segment", "exp", None, None),
        ),
        check_vma=False,
    )
```

profile of v0, /device:TPU:0, one launch (start us, length us, event | category | flops | bytes accessed | tf_op | source)
XLA Modules:
  0.0 517.6 jit_solution(11390773387594596345)
XLA Ops:
  0.6 0.9 fusion.47
  2.0 0.9 reduce-window.14
  2.8 0.2 slice_reduce_fusion.1
  3.3 0.7 all_to_all.32
  4.0 7.3 %all-to-all-start.4 = ((bf16[32,1,1]{2,1,0:T(2,128)(2,1)}), bf16[32,1,1]{2,1,0:T(2,128)(2,1)S(1)}, u32[]{:S(2)}, u32[]{:S(2)}) async-start(bf16[32,1,1]{2,1,0:T(2,128)(2,1)} %all_to_all.32), calls=%async_computation.4 | async-start | bytes 32768 | tf_op jit(solution)/shard_map/all_to_all | solution.py:94
  11.7 1.2 fusion.26
  13.0 0.9 reduce-window.16
  13.9 0.2 slice_reduce_fusion
  14.6 0.2 fusion.29
  14.8 1.2 fusion.28
  16.0 0.7 all_to_all.33
  16.7 1.7 all-to-all-done.4
  18.4 4.1 all-to-all-start.5
  22.5 2.0 convolution_convert_fusion
  24.5 2.8 broadcast_in_dim.81
  27.3 2.3 all-to-all-done.5
  29.6 4.2 broadcast_in_dim.82
  33.8 3.7 all-to-all-start.2
  37.7 0.2 fusion.30
  37.8 2.0 convolution_convert_fusion.1
  39.9 2.8 broadcast_in_dim.78
  42.6 88.7 %all-to-all-done.2 = bf16[32,30,2048]{2,1,0:T(8,128)(2,1)} async-done(((bf16[32,30,2048]{2,1,0:T(8,128)(2,1)}), bf16[32,30,2048]{2,1,0:T(8,128)(2,1)}, u32[]{:S(2)}, u32[]{:S(2)}) %all-to-all-start.2) | async-done | bytes 3932192 | tf_op jit(solution)/shard_map/all_to_all | solution.py:93
  131.3 4.2 broadcast_in_dim.79
  135.5 4.4 all-to-all-start
  139.9 5.0 reshape.171
  144.9 5.4 %fusion.5 = f32[960,704]{0,1:T(8,128)S(1)} fusion(bf16[960,2048]{1,0:T(8,128)(2,1)} %reshape.171, bf16[1,1,704,2048]{3,2,1,0:T(8,128)(2,1)S(1)} %copy-done), kind=kOutput, calls=%fused_computation.16 | convolution fusion | flops 2768240640 | bytes 9519104 | tf_op jit(solution)/shard_map/dot_general | solution.py:103
  150.3 4.5 fusion
  154.9 1.9 collective-permute-start.2
  156.8 3.6 dynamic-slice_bitcast_fusion.1
  160.4 0.2 collective-permute-start.1
  160.6 81.0 %collective-permute-done.2 = bf16[704,960]{1,0:T(8,128)(2,1)} collective-permute-done((bf16[704,960]{1,0:T(8,128)(2,1)}, bf16[704,960]{1,0:T(8,128)(2,1)}, u32[]{:S(2)}, u32[]{:S(2)}) %collective-permute-start.2) | collective-permute-done | bytes 1351712 | tf_op jit(solution)/shard_map/ppermute | solution.py:12
  241.6 2.0 broadcast_select_fusion.1
  243.6 28.4 %collective-permute-done.1 = bf16[704,1024]{1,0:T(8,128)(2,1)} collective-permute-done((bf16[704,1024]{1,0:T(8,128)(2,1)}, bf16[704,1024]{1,0:T(8,128)(2,1)}, u32[]{:S(2)}, u32[]{:S(2)}) %collective-permute-start.1) | collective-permute-done | bytes 1441824 | tf_op jit(solution)/shard_map/ppermute | solution.py:12
  272.0 7.2 %fusion.24 = f32[960,1024]{1,0:T(8,128)} fusion(bf16[704,960]{1,0:T(8,128)(2,1)S(1)} %get-tuple-element.15, bf16[704,960]{1,0:T(8,128)(2,1)S(1)} %get-tuple-element.14, bf16[704,1024]{1,0:T(8,128)(2,1)} %collective-permute-done.1, bf16[704,1024]{1,0:T(8,128)(2,1)S(1)} %copy-done.17, pred[]{:T(512)S(6)} %eq.112), kind=kOutput, calls=%fused_computation.35 | convolution fusion | flops 2786623488 | bytes 9519105 | tf_op jit(solution)/shard_map/dot_general | solution.py:118
  279.2 4.7 reshape.172
  283.9 5.6 %all-to-all-start.3 = ((f32[32,30,1024]{2,1,0:T(8,128)}), f32[32,30,1024]{2,1,0:T(8,128)}, u32[]{:S(2)}, u32[]{:S(2)}) async-start(f32[32,30,1024]{2,1,0:T(8,128)} %reshape.172), calls=%async_computation.3 | async-start | bytes 8388608 | tf_op jit(solution)/shard_map/all_to_all | solution.py:121
  289.5 5.1 reshape.165
  294.6 5.4 %fusion.7 = f32[960,704]{0,1:T(8,128)S(1)} fusion(bf16[960,2048]{1,0:T(8,128)(2,1)} %reshape.165, bf16[1,1,704,2048]{3,2,1,0:T(8,128)(2,1)S(1)} %copy-done), kind=kOutput, calls=%fused_computation.18 | convolution fusion | flops 2768240640 | bytes 9519104 | tf_op jit(solution)/shard_map/dot_general | solution.py:103
  300.1 3.5 fusion.4
  303.6 1.9 collective-permute-start
  305.5 85.1 %collective-permute-done = bf16[704,960]{1,0:T(8,128)(2,1)S(1)} collective-permute-done((bf16[704,960]{1,0:T(8,128)(2,1)S(1)}, bf16[704,960]{1,0:T(8,128)(2,1)S(1)}, u32[]{:S(2)}, u32[]{:S(2)}) %collective-permute-start) | collective-permute-done | bytes 1351712 | tf_op jit(solution)/shard_map/ppermute | solution.py:12
  390.6 0.4 broadcast_select_fusion.3
  391.0 1.1 copy-done.15
  392.1 7.2 %fusion.25 = f32[960,1024]{1,0:T(8,128)} fusion(bf16[704,960]{1,0:T(8,128)(2,1)S(1)} %get-tuple-element.11, bf16[704,960]{1,0:T(8,128)(2,1)S(1)} %get-tuple-element.10, bf16[704,1024]{1,0:T(8,128)(2,1)} %collective-permute-done.1, bf16[704,1024]{1,0:T(8,128)(2,1)S(1)} %copy-done.18, pred[]{:T(512)S(6)} %eq.112), kind=kOutput, calls=%fused_computation.36 | convolution fusion | flops 2786623488 | bytes 9519105 | tf_op jit(solution)/shard_map/dot_general | solution.py:118
  399.3 4.7 reshape.166
  404.0 5.3 %all-to-all-start.1 = ((f32[32,30,1024]{2,1,0:T(8,128)}), f32[32,30,1024]{2,1,0:T(8,128)}, u32[]{:S(2)}, u32[]{:S(2)}) async-start(f32[32,30,1024]{2,1,0:T(8,128)} %reshape.166), calls=%async_computation.1 | async-start | bytes 8388608 | tf_op jit(solution)/shard_map/all_to_all | solution.py:121
  409.3 0.2 fusion.49
  409.7 0.3 select_reduce_fusion
  410.0 0.6 convert_reduce_fusion.3
  410.6 0.6 convert_reduce_fusion.2
  412.6 7.6 %fusion.21 = f32[1024,2048]{1,0:T(8,128)S(1)} fusion(bf16[960,2048]{1,0:T(8,128)(2,1)} %reshape.165, s32[]{:T(128)S(6)} %select_n.61), kind=kOutput, calls=%fused_computation.32 | convolution fusion | flops 4026531840 | bytes 14286852 | tf_op jit(solution)/shard_map/dot_general | solution.py:108
  420.2 7.5 %multiply_bitcast_fusion = f32[1,1,1024,2048]{3,2,1,0:T(8,128)} fusion(f32[1024,2048]{1,0:T(8,128)S(1)} %fusion.21, f32[]{:T(128)S(6)} %div.34, bf16[960,2048]{1,0:T(8,128)(2,1)S(1)} %copy-done.5, s32[]{:T(128)S(6)} %select_n.61), kind=kOutput, calls=%fused_computation | convolution fusion | flops 4030726144 | bytes 22675464 | tf_op jit(solution)/shard_map/dot_general | solution.py:108
  427.7 3.9 fusion.23
  431.7 4.4 multiply_bitcast_fusion.1
  436.1 5.2 %copy.42 = f32[2,2,8,30,1024]{4,1,3,2,0:T(2,128)S(1)} copy(f32[2,2,8,30,1024]{4,3,2,1,0:T(8,128)} %bitcast.14) | data formatting | bytes 7864320 | tf_op jit(solution)/shard_map/reshape | solution.py:129
  441.3 3.7 copy.50
  445.0 58.2 %all-to-all-done.1 = f32[32,30,1024]{2,1,0:T(8,128)} async-done(((f32[32,30,1024]{2,1,0:T(8,128)}), f32[32,30,1024]{2,1,0:T(8,128)}, u32[]{:S(2)}, u32[]{:S(2)}) %all-to-all-start.1) | async-done | bytes 3932192 | tf_op jit(solution)/shard_map/all_to_all | solution.py:121
  503.2 5.5 %copy.38 = f32[2,2,8,30,1024]{4,1,3,2,0:T(2,128)S(1)} copy(f32[2,2,8,30,1024]{4,3,2,1,0:T(8,128)} %bitcast.8) | data formatting | bytes 7864320 | tf_op jit(solution)/shard_map/reshape | solution.py:129
  508.7 1.9 copy.49
  510.6 0.2 copy-done.2
  510.8 2.5 convolution_convert_fusion.2
  513.3 2.5 convolution_convert_fusion.3
  515.8 0.3 multiply_reduce_fusion
  516.1 1.2 convolution_convert_fusion.4
  (82 shorter events, 2.0 us)
Async XLA Ops:
  0.6 144.3 %copy-start = (bf16[1,1,704,2048]{3,2,1,0:T(8,128)(2,1)S(1)}, bf16[1,1,704,2048]{3,2,1,0:T(8,128)(2,1)}, u32[]{:S(2)}) copy-start(bf16[1,1,704,2048]{3,2,1,0:T(8,128)(2,1)} %param.14) | copy-start | bytes 8650756
  4.0 14.4 %all-to-all-start.4 = ((bf16[32,1,1]{2,1,0:T(2,128)(2,1)}), bf16[32,1,1]{2,1,0:T(2,128)(2,1)S(1)}, u32[]{:S(2)}, u32[]{:S(2)}) async-start(bf16[32,1,1]{2,1,0:T(2,128)(2,1)} %all_to_all.32), calls=%async_computation.4 | async-start | bytes 32768 | tf_op jit(solution)/shard_map/all_to_all | solution.py:94
  18.4 11.2 %all-to-all-start.5 = ((bf16[32,1,1]{2,1,0:T(2,128)(2,1)}), bf16[32,1,1]{2,1,0:T(2,128)(2,1)S(1)}, u32[]{:S(2)}, u32[]{:S(2)}) async-start(bf16[32,1,1]{2,1,0:T(2,128)(2,1)} %all_to_all.33), calls=%async_computation.5 | async-start | bytes 32768 | tf_op jit(solution)/shard_map/all_to_all | solution.py:94
  33.8 97.5 %all-to-all-start.2 = ((bf16[32,30,2048]{2,1,0:T(8,128)(2,1)}), bf16[32,30,2048]{2,1,0:T(8,128)(2,1)}, u32[]{:S(2)}, u32[]{:S(2)}) async-start(bf16[32,30,2048]{2,1,0:T(8,128)(2,1)} %bitcast.110), calls=%async_computation.2 | async-start | bytes 8388608 | tf_op jit(solution)/shard_map/all_to_all | solution.py:93
  135.5 148.4 %all-to-all-start = ((bf16[32,30,2048]{2,1,0:T(8,128)(2,1)}), bf16[32,30,2048]{2,1,0:T(8,128)(2,1)}, u32[]{:S(2)}, u32[]{:S(2)}) async-start(bf16[32,30,2048]{2,1,0:T(8,128)(2,1)} %bitcast.109), calls=%async_computation | async-start | bytes 8388608 | tf_op jit(solution)/shard_map/all_to_all | solution.py:93
  144.9 5.4 %copy-start.4 = (bf16[960,2048]{1,0:T(8,128)(2,1)S(1)}, bf16[960,2048]{1,0:T(8,128)(2,1)}, u32[]{:S(2)}) copy-start(bf16[960,2048]{1,0:T(8,128)(2,1)} %reshape.171) | copy-start | bytes 11796484
  144.9 5.5 %copy-start.22 = (bf16[1,1,704,2048]{3,2,1,0:T(8,128)(2,1)S(1)}, bf16[1,1,704,2048]{3,2,1,0:T(8,128)(2,1)}, u32[]{:S(2)}) copy-start(bf16[1,1,704,2048]{3,2,1,0:T(8,128)(2,1)} %param.13) | copy-start | bytes 8650756
  154.9 86.7 %collective-permute-start.2 = (bf16[704,960]{1,0:T(8,128)(2,1)}, bf16[704,960]{1,0:T(8,128)(2,1)}, u32[]{:S(2)}, u32[]{:S(2)}) collective-permute-start(bf16[704,960]{1,0:T(8,128)(2,1)} %fusion), channel_id=1, source_target_pairs={{0,8},{8,0},{16,24},{24,16},{1,9},{9,1},{17,25},{25,17},{2,10},{10... | collective-permute-start | bytes 4055048 | tf_op jit(solution)/shard_map/ppermute | solution.py:12
  160.4 111.6 %collective-permute-start.1 = (bf16[704,1024]{1,0:T(8,128)(2,1)}, bf16[704,1024]{1,0:T(8,128)(2,1)}, u32[]{:S(2)}, u32[]{:S(2)}) collective-permute-start(bf16[704,1024]{1,0:T(8,128)(2,1)} %get-tuple-element.13), channel_id=1, source_target_pairs={{0,8},{8,0},{16,24},{24,16},{1,9},{9,1},{17,25},{25,17},{2,10},{10... | collective-permute-start | bytes 4325384 | tf_op jit(solution)/shard_map/ppermute | solution.py:12
  160.6 111.4 %copy-start.17 = (bf16[704,1024]{1,0:T(8,128)(2,1)S(1)}, bf16[704,1024]{1,0:T(8,128)(2,1)}, u32[]{:S(2)}) copy-start(bf16[704,1024]{1,0:T(8,128)(2,1)} %get-tuple-element.12) | copy-start | bytes 4325380
  243.6 28.4 %copy-start.7 = (bf16[704,960]{1,0:T(8,128)(2,1)}, bf16[704,960]{1,0:T(8,128)(2,1)S(1)}, u32[]{:S(2)}) copy-start(bf16[704,960]{1,0:T(8,128)(2,1)S(1)} %get-tuple-element.14) | copy-start | bytes 4055044
  243.6 28.4 %copy-start.9 = (bf16[704,960]{1,0:T(8,128)(2,1)}, bf16[704,960]{1,0:T(8,128)(2,1)S(1)}, u32[]{:S(2)}) copy-start(bf16[704,960]{1,0:T(8,128)(2,1)S(1)} %get-tuple-element.15) | copy-start | bytes 4055044
  283.9 120.1 %all-to-all-start.3 = ((f32[32,30,1024]{2,1,0:T(8,128)}), f32[32,30,1024]{2,1,0:T(8,128)}, u32[]{:S(2)}, u32[]{:S(2)}) async-start(f32[32,30,1024]{2,1,0:T(8,128)} %reshape.172), calls=%async_computation.3 | async-start | bytes 8388608 | tf_op jit(solution)/shard_map/all_to_all | solution.py:121
  294.6 5.4 %copy-start.6 = (bf16[960,2048]{1,0:T(8,128)(2,1)S(1)}, bf16[960,2048]{1,0:T(8,128)(2,1)}, u32[]{:S(2)}) copy-start(bf16[960,2048]{1,0:T(8,128)(2,1)} %reshape.165) | copy-start | bytes 11796484
  294.6 5.5 %copy-start.23 = (bf16[1,1,704,2048]{3,2,1,0:T(8,128)(2,1)S(1)}, bf16[1,1,704,2048]{3,2,1,0:T(8,128)(2,1)}, u32[]{:S(2)}) copy-start(bf16[1,1,704,2048]{3,2,1,0:T(8,128)(2,1)} %param.13) | copy-start | bytes 8650756
  303.6 87.4 %copy-start.11 = (bf16[704,960]{1,0:T(8,128)(2,1)}, bf16[704,960]{1,0:T(8,128)(2,1)S(1)}, u32[]{:S(2)}) copy-start(bf16[704,960]{1,0:T(8,128)(2,1)S(1)} %fusion.4) | copy-start | bytes 4055044
  303.6 88.5 %copy-start.18 = (bf16[704,1024]{1,0:T(8,128)(2,1)S(1)}, bf16[704,1024]{1,0:T(8,128)(2,1)}, u32[]{:S(2)}) copy-start(bf16[704,1024]{1,0:T(8,128)(2,1)} %get-tuple-element.12) | copy-start | bytes 4325380
  303.6 87.0 %collective-permute-start = (bf16[704,960]{1,0:T(8,128)(2,1)S(1)}, bf16[704,960]{1,0:T(8,128)(2,1)S(1)}, u32[]{:S(2)}, u32[]{:S(2)}) collective-permute-start(bf16[704,960]{1,0:T(8,128)(2,1)S(1)} %fusion.4), channel_id=1, source_target_pairs={{0,8},{8,0},{16,24},{24,16},{1,9},{9,1},{17,25},{25,17},{2,10},{10... | collective-permute-start | bytes 4055048 | tf_op jit(solution)/shard_map/ppermute | solution.py:12
  391.0 1.1 copy-start.15
  391.0 8.3 %copy-start.13 = (bf16[704,960]{1,0:T(8,128)(2,1)}, bf16[704,960]{1,0:T(8,128)(2,1)S(1)}, u32[]{:S(2)}) copy-start(bf16[704,960]{1,0:T(8,128)(2,1)S(1)} %get-tuple-element.10) | copy-start | bytes 4055044
  404.0 5.3 %copy-start.20 = (bf16[2048,16]{0,1:T(8,128)(2,1)S(1)}, bf16[2048,16]{0,1:T(8,128)(2,1)}, u32[]{:S(2)}) copy-start(bf16[2048,16]{0,1:T(8,128)(2,1)} %param.11) | copy-start | bytes 196612
  404.0 5.5 %copy-start.21 = (s32[128,6]{0,1:T(8,128)S(1)}, s32[128,6]{0,1:T(8,128)}, u32[]{:S(2)}) copy-start(s32[128,6]{0,1:T(8,128)} %param.12) | copy-start | bytes 9220
  404.0 99.2 %all-to-all-start.1 = ((f32[32,30,1024]{2,1,0:T(8,128)}), f32[32,30,1024]{2,1,0:T(8,128)}, u32[]{:S(2)}, u32[]{:S(2)}) async-start(f32[32,30,1024]{2,1,0:T(8,128)} %reshape.166), calls=%async_computation.1 | async-start | bytes 8388608 | tf_op jit(solution)/shard_map/all_to_all | solution.py:121
  412.6 7.6 %copy-start.5 = (bf16[960,2048]{1,0:T(8,128)(2,1)S(1)}, bf16[960,2048]{1,0:T(8,128)(2,1)}, u32[]{:S(2)}) copy-start(bf16[960,2048]{1,0:T(8,128)(2,1)} %reshape.171) | copy-start | bytes 11796484
  420.2 7.5 %copy-start.8 = (bf16[704,960]{1,0:T(8,128)(2,1)S(1)}, bf16[704,960]{1,0:T(8,128)(2,1)}, u32[]{:S(2)}) copy-start(bf16[704,960]{1,0:T(8,128)(2,1)} %copy-done.7) | copy-start | bytes 4055044
  420.2 7.5 %copy-start.10 = (bf16[704,960]{1,0:T(8,128)(2,1)S(1)}, bf16[704,960]{1,0:T(8,128)(2,1)}, u32[]{:S(2)}) copy-start(bf16[704,960]{1,0:T(8,128)(2,1)} %copy-done.9) | copy-start | bytes 4055044
  427.7 4.0 copy-start.12
  427.7 4.0 copy-start.14
  427.7 4.0 copy-start.16
  508.7 2.1 copy-start.2
  513.3 2.5 copy-start.3
  513.3 2.8 copy-start.24
  513.3 2.8 copy-start.25
  513.3 4.0 copy-start.1
  516.1 1.2 copy-start.19
where the time goes:
time: 523 us; the launch traced here: 518 us
  waiting for transfers between devices  345 us (66%)
  matrix products  67.1 us (13%)
  local copies, waits for them, and re-layouts  58.8 us (11%)
  starting transfers between devices  34.3 us (7%)
  other arithmetic  9.21 us (2%)
    ppermute x3, waiting for transfers between devices, swapped(): return lax.ppermute(value, axis, pairs)  195 us
    all_to_all x2, waiting for transfers between devices, body(): lax.all_to_all(grid_rows, ('segment', 'exp'), split_axis=0, concat_axis=0...  88.7 us
    all_to_all x2, waiting for transfers between devices, body(): lax.all_to_all(column_half.reshape(devices, capacity, width_half), ('segm...  58.2 us
    dot_general x2, matrix products, body(): lax.dot_general(own_columns, received, (((0,), (0,)), ((), ())), preferre...  15 us
    dot_general x2, matrix products, body(): lax.dot_general(full_hidden, down_block, (((0,), (0,)), ((), ())), prefer...  14.4 us
    broadcast_in_dim x4, local copies, waits for them, and re-layouts, body(): jnp.broadcast_to(buffer.reshape(pair_count, 1, columns, capacity, model_w...  13.9 us
    all_to_all x2, starting transfers between devices, body(): lax.all_to_all(grid_counts, ('segment', 'exp'), split_axis=0, concat_axis...  11.4 us
    all_to_all x2, starting transfers between devices, body(): lax.all_to_all(column_half.reshape(devices, capacity, width_half), ('segm...  10.9 us
  transfers between devices with their start and end apart: 9, of which 7 were waited for; matrix products, arithmetic and copies ran while one was open for 21% of the time, Pallas kernels for 0%

commit v1 on v0

--- a/solution.py
+++ b/solution.py
@@ -17,7 +17,7 @@
     return values * lax.rsqrt(mean_square + 1e-06) * gain
 
 
-def body(
+def dispatch_body(
     hidden_rows,
     norm_gain,
     router_weight,
@@ -66,6 +66,8 @@
     count_total = jnp.zeros((), jnp.float32)
     mix_blocks = []
     positions = jnp.arange(experts * capacity, dtype=jnp.int32)
+    pair_rows = jnp.arange(micro_rows * top_count, dtype=jnp.int32)
+    earlier = (pair_rows[:, None] > pair_rows[None, :]).astype(jnp.bfloat16)
     for step_index in range(tok_rows // micro_rows):
         low = step_index * micro_rows
         block_rows = normed[low : low + micro_rows]
@@ -73,7 +75,10 @@
         block_gates = gate_share[low : low + micro_rows]
         flat_ids = block_ids.reshape(-1)
         onehot = (flat_ids[:, None] == expert_grid[None, :]).astype(jnp.int32)
-        slot_rank = jnp.sum((jnp.cumsum(onehot, axis=0) - onehot) * onehot, axis=1)
+        before = jnp.dot(
+            earlier, onehot.astype(jnp.bfloat16), preferred_element_type=jnp.float32
+        ).astype(jnp.int32)
+        slot_rank = jnp.sum(before * onehot, axis=1)
         target = (flat_ids * capacity + slot_rank).reshape(micro_rows, top_count)
         picker = target[:, :, None] == positions[None, None, :]
         dispatch_table = jnp.any(picker, axis=1).astype(jnp.bfloat16)
@@ -149,9 +154,131 @@
     return (expert_mix, latents, gram_input, gram_hidden)
 
 
+GROUP = 512
+
+
+def exchanged(value, axis, mask):
+    pairs = [(source, source ^ mask) for source in range(lax.axis_size(axis))]
+    return lax.ppermute(value, axis, pairs)
+
+
+def halve(value, dim, bit, axis, mask):
+    kept = lax.dynamic_index_in_dim(value, bit, dim, keepdims=False)
+    sent = lax.dynamic_index_in_dim(value, 1 - bit, dim, keepdims=False)
+    came = exchanged(sent.astype(jnp.bfloat16), axis, mask)
+    return kept.astype(jnp.float32) + came.astype(jnp.float32)
+
+
+def gate_table(normed, router_weight, expert_ids):
+    experts = router_weight.shape[1]
+    logits = jnp.dot(normed, router_weight, preferred_element_type=jnp.float32)
+    grid = jnp.arange(experts, dtype=jnp.int32)
+    choose = jnp.any(expert_ids[:, :, None] == grid[None, None, :], axis=1)
+    affinity = jnp.where(choose, jax.nn.sigmoid(logits), 0.0)
+    share = affinity / jnp.sum(affinity, axis=1, keepdims=True)
+    return jnp.where(choose, share, -1.0)
+
+
+def gather_body(
+    hidden_rows,
+    norm_gain,
+    router_weight,
+    expert_ids,
+    gate_weight,
+    up_weight,
+    down_weight,
+    latent_gain,
+    kv_weight,
+):
+    segment = lax.axis_index("segment")
+    column = lax.axis_index("exp")
+    columns = lax.axis_size("exp")
+    half_index = segment % 2
+    expert = (segment // 2) * columns + column
+    core, along_x, along_y = column % 2, (column // 2) % 2, column // 4
+    tok_rows, model_width = hidden_rows.shape
+    width_half = model_width // 2
+    experts = router_weight.shape[1]
+    capacity = GROUP * expert_ids.shape[1] * 5 // (4 * experts)
+    w_gate, w_up, w_down = gate_weight[0, 0], up_weight[0, 0], down_weight[0, 0]
+    half_units = w_gate.shape[0]
+
+    residual = hidden_rows.astype(jnp.float32)
+    normed = rms_norm(residual, norm_gain).astype(jnp.bfloat16)
+    table = gate_table(normed, router_weight, expert_ids)
+    everywhere = ("segment", "exp")
+    all_table = lax.all_gather(table, everywhere, axis=0, tiled=True)
+    all_rows = lax.all_gather(normed, everywhere, axis=0, tiled=True)
+
+    own = jnp.arange(experts, dtype=jnp.int32) == expert
+    gates = jnp.sum(jnp.where(own[None, :], all_table, 0.0), axis=1).reshape(-1, GROUP)
+    named = gates >= 0.0
+    count = jnp.sum(named.astype(jnp.float32))
+    place = jnp.arange(GROUP, dtype=jnp.int32)
+    earlier = (place[:, None] < place[None, :]).astype(jnp.bfloat16)
+    rank = jnp.dot(named.astype(jnp.bfloat16), earlier, preferred_element_type=jnp.float32)
+    rank = jnp.where(named, rank.astype(jnp.int32), -1)
+    slots = jnp.arange(capacity, dtype=jnp.int32)
+    picks = rank[:, None, :] == slots[None, :, None]
+    slot_gates = jnp.sum(jnp.where(picks, gates[:, None, :], 0.0), axis=2)
+    picks = picks.astype(jnp.bfloat16)
+    groups = picks.shape[0]
+
+    rows = lax.dot_general(
+        picks,
+        all_rows.reshape(groups, GROUP, model_width),
+        (((2,), (1,)), ((0,), (0,))),
+        preferred_element_type=jnp.float32,
+    ).astype(jnp.bfloat16)
+    rows = rows.reshape(groups * capacity, model_width)
+    by_units = (((1,), (1,)), ((), ()))
+    gate_pre = lax.dot_general(rows, w_gate, by_units, preferred_element_type=jnp.float32)
+    up_pre = lax.dot_general(rows, w_up, by_units, preferred_element_type=jnp.float32)
+    hidden = (jax.nn.silu(gate_pre) * up_pre).astype(jnp.bfloat16)
+    other_hidden = exchanged(hidden, "segment", 1)
+    out = jnp.dot(hidden, w_down, preferred_element_type=jnp.float32)
+    out = (out * slot_gates.reshape(-1, 1)).astype(jnp.bfloat16)
+    mix = lax.dot_general(
+        picks,
+        out.reshape(groups, capacity, model_width),
+        (((1,), (1,)), ((0,), (0,))),
+        preferred_element_type=jnp.float32,
+    ).astype(jnp.bfloat16)
+    mix = mix.reshape(2, 2, 2, 2, 2, tok_rows, model_width)
+    mix = halve(mix, 4, core, "exp", 1)
+    first = halve(mix[..., :width_half], 3, along_x, "exp", 2)
+    second = halve(mix[..., width_half:], 2, along_y, "exp", 4)
+    first = halve(first, 2, along_y, "exp", 4)
+    second = halve(second, 2, along_x, "exp", 2)
+    mix = jnp.concatenate([first, second], axis=-1)
+    mix = halve(mix, 0, segment // 2, "segment", 2)
+    mix = halve(mix, 0, segment % 2, "segment", 1)
+
+    expert_mix = mix.astype(jnp.bfloat16)
+    combined = residual + expert_mix.astype(jnp.float32)
+    normed_next = rms_norm(combined, latent_gain).astype(jnp.bfloat16)
+    latents = jnp.dot(normed_next, kv_weight, preferred_element_type=jnp.float32).astype(
+        jnp.bfloat16
+    )
+    by_slots = (((0,), (0,)), ((), ()))
+    inverse_count = 2.0 / count
+    own_columns = lax.dynamic_slice_in_dim(rows, half_index * width_half, width_half, 1)
+    gram_in = lax.dot_general(own_columns, rows, by_slots, preferred_element_type=jnp.float32)
+    first_half = jnp.where(half_index == 0, hidden, other_hidden)
+    second_half = jnp.where(half_index == 0, other_hidden, hidden)
+    full_hidden = jnp.concatenate([first_half, second_half], axis=1)
+    gram_hid = lax.dot_general(hidden, full_hidden, by_slots, preferred_element_type=jnp.float32)
+    return (
+        expert_mix,
+        latents,
+        (gram_in * inverse_count)[None, None],
+        (gram_hid * inverse_count)[None, None],
+    )
+
+
 def solution(mesh):
     return jax.shard_map(
-        body,
+        gather_body if mesh.shape["exp"] == 8 and mesh.shape["segment"] == 4 else dispatch_body,
         mesh=mesh,
         in_specs=(
             P(("segment", "exp"), None),

time: 523 us -> 389 us (0.74); the launches traced: 518 us -> 389 us
  waiting for transfers between devices: 345 us -> 192 us
  blocking collectives: 0 us -> 44.9 us
  starting transfers between devices: 34.3 us -> 7.01 us
  local copies, waits for them, and re-layouts: 58.8 us -> 36.1 us
  other arithmetic: 9.21 us -> 27 us
  between operations: 2.78 us -> 15.1 us
    all_to_all x6 -> x0, waiting for transfers between devices: 151 us -> none  [the longest x2 88.7 us: body(): lax.all_to_all(grid_rows, ('segment', 'exp'), split_axis=0, concat_axis=0...]
    ppermute x3 -> x8, waiting for transfers between devices: 195 us -> 121 us  [exchanged(): return lax.ppermute(value, axis, pairs)]
    all_gather x0 -> x1, waiting for transfers between devices: none -> 71 us  [gather_body(): all_rows = lax.all_gather(normed, everywhere, axis=0, tiled=True)]
    all_gather x0 -> x1, blocking collectives: none -> 44.9 us  [gather_body(): all_table = lax.all_gather(table, everywhere, axis=0, tiled=True)]
    all_to_all x6 -> x0, starting transfers between devices: 30.3 us -> none  [the longest x2 11.4 us: body(): lax.all_to_all(grid_counts, ('segment', 'exp'), split_axis=0, concat_axis...]
    reshape x6 -> x1, local copies, waits for them, and re-layouts: 30.1 us -> 0.01 us  [gather_body(): jnp.sum(jnp.where(own[None, :], all_table, 0.0), axis=1).reshape(-1, GROUP)]
    add x2 -> x6, other arithmetic: 0.01 us -> 18.8 us  [halve(): return kept.astype(jnp.float32) + came.astype(jnp.float32)]
    dynamic_slice x1 -> x2, local copies, waits for them, and re-layouts: 3.64 us -> 20.3 us  [the longest x1 12 us: halve(): kept = lax.dynamic_index_in_dim(value, bit, dim, keepdims=False)]
  transfers between devices with their start and end apart: 9 -> 9, of which waited for: 7 -> 8; matrix products, arithmetic and copies ran while one was open for 21% -> 12% of each run, Pallas kernels for 0% -> 0%
where the time goes in v1:
time: 389 us
  waiting for transfers between devices  192 us (49%)
  matrix products  66.9 us (17%)
  blocking collectives  44.9 us (12%)
  local copies, waits for them, and re-layouts  36.1 us (9%)
  other arithmetic  27 us (7%)
  between operations  15.1 us (4%)
  starting transfers between devices  7.01 us (2%)
    ppermute x8, waiting for transfers between devices, exchanged(): return lax.ppermute(value, axis, pairs)  121 us
    all_gather x1, waiting for transfers between devices, gather_body(): all_rows = lax.all_gather(normed, everywhere, axis=0, tiled=True)  71 us
    all_gather x1, blocking collectives, gather_body(): all_table = lax.all_gather(table, everywhere, axis=0, tiled=True)  44.9 us
    add x6, other arithmetic, halve(): return kept.astype(jnp.float32) + came.astype(jnp.float32)  18.8 us
    dot_general x1, matrix products, gather_body(): lax.dot_general(own_columns, rows, by_slots, preferred_element_type=jnp.f...  14.5 us
    dynamic_slice x1, local copies, waits for them, and re-layouts, halve(): kept = lax.dynamic_index_in_dim(value, bit, dim, keepdims=False)  12 us
    dot_general x1, matrix products, gather_body(): lax.dot_general(picks, all_rows.reshape(groups, GROUP, model_width), (((2...  10.6 us
    dot_general x1, matrix products, gather_body(): lax.dot_general(hidden, full_hidden, by_slots, preferred_element_type=jnp...  8.47 us
  transfers between devices with their start and end apart: 9, of which 8 were waited for; matrix products, arithmetic and copies ran while one was open for 12% of the time, Pallas kernels for 0%

profile of v1, /device:TPU:0, one launch (start us, length us, event | category | flops | bytes accessed | tf_op | source)
XLA Modules:
  0.0 389.0 jit_solution(4781425730085573977)
XLA Ops:
  7.2 0.0 copy-start
  7.2 0.0 all-gather.2.cloned.1.call-start
  7.2 1.4 fusion.25
  8.6 2.0 fusion.27
  10.6 0.0 all-gather.2.cloned.1.call-update
  10.7 0.7 fusion.35
  11.4 1.3 fusion.43
  12.7 44.9 %all_gather.6 = f32[4096,16]{0,1:T(8,128)S(1)} all-gather(f32[128,16]{0,1:T(8,128)S(1)} %divide_select_fusion), channel_id=1, replica_groups=mesh['segment'=4,'exp'=8] {'segment','exp'}, dimensions={0}, use_global_device_ids=true | all-gather | bytes 270336 | tf_op jit(solution)/shard_map/all_gather | solution.py:210
  57.7 0.1 select_reduce_fusion.1
  57.8 0.2 fusion.20
  58.0 0.5 select_reduce_fusion
  58.4 0.1 mul.81
  58.5 71.0 %all-gather.2.cloned.1.call-done = bf16[4096,2048]{1,0:T(8,128)(2,1)} async-done(((bf16[128,2048]{1,0:T(8,128)(2,1)}), bf16[4096,2048]{1,0:T(8,128)(2,1)}) %all-gather.2.cloned.1.call-update) | async-done | bytes 16777232 | tf_op jit(solution)/shard_map/all_gather | solution.py:211
  129.6 10.6 %convolution_convert_fusion.1 = bf16[8,240,2048]{2,1,0:T(8,128)(2,1)S(1)} fusion(bf16[8,512,2048]{2,1,0:T(8,128)(2,1)} %bitcast.65, s32[8,512]{1,0:T(8,128)S(1)} %fusion.20), kind=kOutput, calls=%fused_computation.11 | convolution fusion | flops 4031447040 | bytes 24657920 | tf_op jit(solution)/shard_map/dot_general | solution.py:227
  140.2 0.0 copy-start.9
  140.2 6.2 %fusion.9 = f32[1920,704]{0,1:T(8,128)S(1)} fusion(bf16[1920,2048]{1,0:T(8,128)(2,1)S(1)} %bitcast.67, bf16[1,1,704,2048]{3,2,1,0:T(8,128)(2,1)S(1)} %copy-done.8), kind=kOutput, calls=%fused_computation.26 | convolution fusion | flops 5536481280 | bytes 16154624 | tf_op jit(solution)/shard_map/dot_general | solution.py:235
  146.4 8.0 %multiply_convert_fusion.1 = bf16[1920,704]{0,1:T(8,128)(2,1)} fusion(f32[1920,704]{0,1:T(8,128)S(1)} %fusion.9, bf16[1920,2048]{1,0:T(8,128)(2,1)S(1)} %bitcast.68, bf16[1,1,704,2048]{3,2,1,0:T(8,128)(2,1)S(1)} %copy-done.9), kind=kOutput, calls=%fused_computation.10 | convolution fusion | flops 5544591360 | bytes 18857984 | tf_op jit(solution)/shard_map/dot_general | solution.py:236
  154.4 8.3 %multiply_convert_fusion = bf16[1920,2048]{1,0:T(8,128)(2,1)S(1)} fusion(bf16[1920,704]{0,1:T(8,128)(2,1)} %multiply_convert_fusion.1, f32[1920]{0:T(1024)S(1)} %mul.81, bf16[1,1,704,2048]{3,2,1,0:T(8,128)(2,1)S(1)} %copy-done), kind=kOutput, calls=%fused_computation.1 | convolution fusion | flops 5544345600 | bytes 13458944 | tf_op jit(solution)/shard_map/dot_general | solution.py:239
  162.7 8.2 %convolution_convert_fusion = bf16[8,512,2048]{2,1,0:T(8,128)(2,1)} fusion(bf16[8,240,2048]{2,1,0:T(8,128)(2,1)S(1)} %bitcast.70, s32[8,512]{1,0:T(8,128)S(1)} %fusion.20), kind=kOutput, calls=%fused_computation.2 | convolution fusion | flops 4035903488 | bytes 24657920 | tf_op jit(solution)/shard_map/dot_general | solution.py:241
  170.9 12.0 %constant_dynamic-slice_fusion.1 = (bf16[2,2,2,2,1,128,2048]{6,5,4,3,2,1,0:T(8,128)(2,1)}, bf16[2,2,2,2,1,128,2048]{6,5,4,3,2,1,0:T(8,128)(2,1)}) fusion(bf16[2,2,2,2,2,128,2048]{6,5,4,3,2,1,0:T(8,128)(2,1)} %bitcast.64, s32[]{:T(128)S(6)} %select_n.109, s32[]{:T(128)S(6)} %select_n.110), kind=kLoop, calls=%fused_computation.78 | loop fusion | bytes 33554440 | tf_op jit(solution)/shard_map/jit(dynamic_index_in_dim)/dynamic_slice | solution.py:166
  182.9 8.3 %copy.23 = bf16[2,2,2,2,1,128,2048]{6,5,1,0,3,2,4:T(8,128)(2,1)} copy(bf16[2,2,2,2,1,128,2048]{6,5,4,3,2,1,0:T(8,128)(2,1)} %get-tuple-element.9) | data formatting | bytes 16777216 | tf_op jit(solution)/shard_map/jit(dynamic_index_in_dim)/dynamic_slice | solution.py:167
  191.2 0.3 collective-permute-start
  191.5 13.2 %collective-permute-done = bf16[2,2,2,2,128,2048]{5,4,1,0,3,2:T(8,128)(2,1)} collective-permute-done((bf16[2,2,2,2,128,2048]{5,4,1,0,3,2:T(8,128)(2,1)}, bf16[2,2,2,2,128,2048]{5,4,1,0,3,2:T(8,128)(2,1)}, u32[]{:S(2)}, u32[]{:S(2)}) %collective-permute-start) | collective-permute-done | bytes 8388640 | tf_op jit(solution)/shard_map/ppermute | solution.py:162
  204.7 7.6 %convert_add_fusion = f32[2,2,2,2,128,2048]{5,4,1,0,3,2:T(8,128)S(1)} fusion(bf16[2,2,2,2,128,2048]{5,4,1,0,3,2:T(8,128)(2,1)} %collective-permute-done, bf16[2,2,2,2,1,128,2048]{6,5,4,3,2,1,0:T(8,128)(2,1)} %get-tuple-element.8), kind=kLoop, calls=%fused_computation | loop fusion | flops 12582912 | bytes 33554432 | tf_op jit(solution)/shard_map/add | solution.py:169
  212.3 6.8 %fusion.42 = (f32[2,2,2,2,128,1024]{5,4,1,0,3,2:T(8,128)}, f32[2,2,2,2,128,1024]{5,4,1,0,3,2:T(8,128)}) fusion(f32[2,2,2,2,128,2048]{5,4,1,0,3,2:T(8,128)S(1)} %convert_add_fusion), kind=kLoop, calls=%fused_computation.84 | loop fusion | bytes 33554432 | tf_op jit(solution)/shard_map/slice | solution.py:250
  219.1 2.5 fusion.12
  221.6 1.5 collective-permute-start.3
  223.1 3.8 fusion.11
  227.0 0.6 collective-permute-start.1
  227.5 42.0 %collective-permute-done.3 = bf16[2,2,2,128,1024]{4,3,1,0,2:T(8,128)(2,1)} collective-permute-done((bf16[2,2,2,128,1024]{4,3,1,0,2:T(8,128)(2,1)S(1)}, bf16[2,2,2,128,1024]{4,3,1,0,2:T(8,128)(2,1)}, u32[]{:S(2)}, u32[]{:S(2)}) %collective-permute-start.3) | collective-permute-done | bytes 2097184 | tf_op jit(solution)/shard_map/ppermute | solution.py:162
  269.5 3.5 bitcast_add_fusion
  273.1 0.2 fusion.29
  273.2 1.3 collective-permute-start.4
  274.6 0.2 collective-permute-done.1
  274.8 3.5 bitcast_add_fusion.1
  278.3 0.0 copy-start.3
  278.3 1.2 fusion.28
  279.6 1.1 copy-done.3
  280.6 1.2 collective-permute-start.2
  281.8 0.6 convert_reduce_fusion
  283.1 0.0 copy-start.4
  283.2 0.5 collective-permute-start.7
  283.6 14.3 %collective-permute-done.4 = bf16[2,2,128,1024]{3,2,1,0:T(8,128)(2,1)} collective-permute-done((bf16[2,2,128,1024]{3,2,1,0:T(8,128)(2,1)S(1)}, bf16[2,2,128,1024]{3,2,1,0:T(8,128)(2,1)}, u32[]{:S(2)}, u32[]{:S(2)}) %collective-permute-start.4) | collective-permute-done | bytes 1048608 | tf_op jit(solution)/shard_map/ppermute | solution.py:162
  297.9 2.4 bitcast_add_fusion.2
  300.3 4.9 %collective-permute-done.2 = bf16[2,2,128,1024]{3,2,1,0:T(8,128)(2,1)} collective-permute-done((bf16[2,2,128,1024]{3,2,1,0:T(8,128)(2,1)}, bf16[2,2,128,1024]{3,2,1,0:T(8,128)(2,1)}, u32[]{:S(2)}, u32[]{:S(2)}) %collective-permute-start.2) | collective-permute-done | bytes 1048608 | tf_op jit(solution)/shard_map/ppermute | solution.py:162
  305.2 1.6 bitcast_add_fusion.3
  306.7 0.1 fusion.30
  306.9 1.6 collective-permute-start.5
  308.5 14.5 %multiply_bitcast_fusion = f32[1,1,1024,2048]{3,2,1,0:T(8,128)} fusion(bf16[1920,2048]{1,0:T(8,128)(2,1)} %bitcast.69, f32[]{:T(128)S(6)} %div.62, s32[]{:T(128)S(6)} %select_n.123), kind=kOutput, calls=%fused_computation.5 | convolution fusion | flops 8055160832 | bytes 20185096 | tf_op jit(solution)/shard_map/dot_general | solution.py:266
  322.9 42.7 %collective-permute-done.7 = bf16[1920,704]{0,1:T(8,128)(2,1)S(1)} collective-permute-done((bf16[1920,704]{0,1:T(8,128)(2,1)}, bf16[1920,704]{0,1:T(8,128)(2,1)S(1)}, u32[]{:S(2)}, u32[]{:S(2)}) %collective-permute-start.7) | collective-permute-done | bytes 2703392 | tf_op jit(solution)/shard_map/ppermute | solution.py:162
  365.6 2.4 broadcast_select_fusion.1
  368.0 0.0 collective-permute-done.5
  368.0 0.3 fusion.17
  368.3 0.1 fusion.32
  368.4 0.1 collective-permute-start.6
  368.5 0.0 copy-start.6
  368.5 0.0 copy-start.10
  368.5 0.0 copy-start.11
  368.5 0.0 copy-start.1
  368.5 8.5 %multiply_bitcast_fusion.1 = f32[1,1,704,1408]{3,2,1,0:T(8,128)} fusion(bf16[1920,704]{0,1:T(8,128)(2,1)} %multiply_convert_fusion.1, bf16[1920,704]{0,1:T(8,128)(2,1)S(1)} %get-tuple-element.11, bf16[1920,704]{0,1:T(8,128)(2,1)S(1)} %get-tuple-element.10, f32[]{:T(128)S(6)} %div.62), kind=kOutput, calls=%fused_computation.20 | convolution fusion | flops 3818135552 | bytes 12075012 | tf_op jit(solution)/shard_map/dot_general | solution.py:270
  377.0 3.6 collective-permute-done.6
  380.6 0.3 multiply_reduce_fusion
  380.9 0.0 copy-start.7
  380.9 1.2 convolution_convert_fusion.2
  (19 shorter events, 0.1 us)
Async XLA Ops:
  7.2 147.2 %copy-start = (bf16[1,1,704,2048]{3,2,1,0:T(8,128)(2,1)S(1)}, bf16[1,1,704,2048]{3,2,1,0:T(8,128)(2,1)}, u32[]{:S(2)}) copy-start(bf16[1,1,704,2048]{3,2,1,0:T(8,128)(2,1)} %param.15) | copy-start | bytes 8650756
  7.2 122.4 %all-gather.2.cloned.1.call-start = ((), (), s32[]{:S(2)}) async-start(), calls=%async_computation | async-start | bytes 17301504 | tf_op jit(solution)/shard_map/all_gather | solution.py:211
  129.6 10.6 %copy-start.8 = (bf16[1,1,704,2048]{3,2,1,0:T(8,128)(2,1)S(1)}, bf16[1,1,704,2048]{3,2,1,0:T(8,128)(2,1)}, u32[]{:S(2)}) copy-start(bf16[1,1,704,2048]{3,2,1,0:T(8,128)(2,1)} %param.13) | copy-start | bytes 8650756
  140.2 6.2 %copy-start.5 = (bf16[8,240,2048]{2,1,0:T(8,128)(2,1)}, bf16[8,240,2048]{2,1,0:T(8,128)(2,1)S(1)}, u32[]{:S(2)}) copy-start(bf16[8,240,2048]{2,1,0:T(8,128)(2,1)S(1)} %convolution_convert_fusion.1) | copy-start | bytes 23592964
  140.2 6.2 %copy-start.9 = (bf16[1,1,704,2048]{3,2,1,0:T(8,128)(2,1)S(1)}, bf16[1,1,704,2048]{3,2,1,0:T(8,128)(2,1)}, u32[]{:S(2)}) copy-start(bf16[1,1,704,2048]{3,2,1,0:T(8,128)(2,1)} %param.14) | copy-start | bytes 8650756
  191.2 13.5 %collective-permute-start = (bf16[2,2,2,2,128,2048]{5,4,1,0,3,2:T(8,128)(2,1)}, bf16[2,2,2,2,128,2048]{5,4,1,0,3,2:T(8,128)(2,1)}, u32[]{:S(2)}, u32[]{:S(2)}) collective-permute-start(bf16[2,2,2,2,128,2048]{5,4,1,0,3,2:T(8,128)(2,1)} %bitcast.66), channel_id=1, source_target_pairs={{0,1},{1,0},{2,3},{3,2},{4,5},{5,4},{6,7},{7,6},{8,9},{9,8},{10,11... | collective-permute-start | bytes 25165832 | tf_op jit(solution)/shard_map/ppermute | solution.py:162
  221.6 48.0 %collective-permute-start.3 = (bf16[2,2,2,128,1024]{4,3,1,0,2:T(8,128)(2,1)S(1)}, bf16[2,2,2,128,1024]{4,3,1,0,2:T(8,128)(2,1)}, u32[]{:S(2)}, u32[]{:S(2)}) collective-permute-start(bf16[2,2,2,128,1024]{4,3,1,0,2:T(8,128)(2,1)S(1)} %fusion.12), channel_id=1, source_target_pairs={{0,4},{1,5},{2,6},{3,7},{4,0},{5,1},{6,2},{7,3},{8,12},{9,13},{10,... | collective-permute-start | bytes 6291464 | tf_op jit(solution)/shard_map/ppermute | solution.py:162
  227.0 47.8 %collective-permute-start.1 = (bf16[2,2,2,128,1024]{4,3,1,0,2:T(8,128)(2,1)}, bf16[2,2,2,128,1024]{4,3,1,0,2:T(8,128)(2,1)}, u32[]{:S(2)}, u32[]{:S(2)}) collective-permute-start(bf16[2,2,2,128,1024]{4,3,1,0,2:T(8,128)(2,1)} %fusion.11), channel_id=1, source_target_pairs={{0,2},{1,3},{2,0},{3,1},{4,6},{5,7},{6,4},{7,5},{8,10},{9,11},{10,... | collective-permute-start | bytes 6291464 | tf_op jit(solution)/shard_map/ppermute | solution.py:162
  273.1 5.3 %copy-start.2 = (f32[2,2,2,128,1024]{4,3,1,0,2:T(8,128)}, f32[2,2,2,128,1024]{4,3,1,0,2:T(8,128)S(1)}, u32[]{:S(2)}) copy-start(f32[2,2,2,128,1024]{4,3,1,0,2:T(8,128)S(1)} %bitcast_add_fusion) | copy-start | bytes 12582916
  273.2 24.7 %collective-permute-start.4 = (bf16[2,2,128,1024]{3,2,1,0:T(8,128)(2,1)S(1)}, bf16[2,2,128,1024]{3,2,1,0:T(8,128)(2,1)}, u32[]{:S(2)}, u32[]{:S(2)}) collective-permute-start(bf16[2,2,128,1024]{3,2,1,0:T(8,128)(2,1)S(1)} %fusion.29), channel_id=1, source_target_pairs={{0,2},{1,3},{2,0},{3,1},{4,6},{5,7},{6,4},{7,5},{8,10},{9,11},{10,... | collective-permute-start | bytes 3145736 | tf_op jit(solution)/shard_map/ppermute | solution.py:162
  278.3 2.3 copy-start.3
  280.6 24.5 %collective-permute-start.2 = (bf16[2,2,128,1024]{3,2,1,0:T(8,128)(2,1)}, bf16[2,2,128,1024]{3,2,1,0:T(8,128)(2,1)}, u32[]{:S(2)}, u32[]{:S(2)}) collective-permute-start(bf16[2,2,128,1024]{3,2,1,0:T(8,128)(2,1)} %fusion.28), channel_id=1, source_target_pairs={{0,4},{1,5},{2,6},{3,7},{4,0},{5,1},{6,2},{7,3},{8,12},{9,13},{10,... | collective-permute-start | bytes 3145736 | tf_op jit(solution)/shard_map/ppermute | solution.py:162
  283.1 22.0 %copy-start.4 = (f32[2,2,2,128,1024]{4,3,1,0,2:T(8,128)S(1)}, f32[2,2,2,128,1024]{4,3,1,0,2:T(8,128)}, u32[]{:S(2)}) copy-start(f32[2,2,2,128,1024]{4,3,1,0,2:T(8,128)} %copy-done.3) | copy-start | bytes 12582916
  283.2 82.5 %collective-permute-start.7 = (bf16[1920,704]{0,1:T(8,128)(2,1)}, bf16[1920,704]{0,1:T(8,128)(2,1)S(1)}, u32[]{:S(2)}, u32[]{:S(2)}) collective-permute-start(bf16[1920,704]{0,1:T(8,128)(2,1)} %multiply_convert_fusion.1), channel_id=1, source_target_pairs={{0,8},{8,0},{16,24},{24,16},{1,9},{9,1},{17,25},{25,17},{2,10},{10... | collective-permute-start | bytes 8110088 | tf_op jit(solution)/shard_map/ppermute | solution.py:162
  306.9 61.1 %collective-permute-start.5 = (bf16[2,128,2048]{2,1,0:T(8,128)(2,1)S(1)}, bf16[2,128,2048]{2,1,0:T(8,128)(2,1)S(1)}, u32[]{:S(2)}, u32[]{:S(2)}) collective-permute-start(bf16[2,128,2048]{2,1,0:T(8,128)(2,1)S(1)} %fusion.30), channel_id=1, source_target_pairs={{0,16},{8,24},{16,0},{24,8},{1,17},{9,25},{17,1},{25,9},{2,18},{10... | collective-permute-start | bytes 3145736 | tf_op jit(solution)/shard_map/ppermute | solution.py:162
  368.4 12.2 %collective-permute-start.6 = (bf16[128,2048]{1,0:T(8,128)(2,1)S(1)}, bf16[128,2048]{1,0:T(8,128)(2,1)S(1)}, u32[]{:S(2)}, u32[]{:S(2)}) collective-permute-start(bf16[128,2048]{1,0:T(8,128)(2,1)S(1)} %fusion.32), channel_id=1, source_target_pairs={{0,8},{8,0},{16,24},{24,16},{1,9},{9,1},{17,25},{25,17},{2,10},{10... | collective-permute-start | bytes 1572872 | tf_op jit(solution)/shard_map/ppermute | solution.py:162
  368.5 12.1 %copy-start.6 = (bf16[128,2048]{1,0:T(8,128)(2,1)S(1)}, bf16[128,2048]{1,0:T(8,128)(2,1)}, u32[]{:S(2)}) copy-start(bf16[128,2048]{1,0:T(8,128)(2,1)} %param.9) | copy-start | bytes 1572868
  368.5 12.4 %copy-start.10 = (bf16[2048,512]{1,0:T(8,128)(2,1)S(1)}, bf16[2048,512]{1,0:T(8,128)(2,1)}, u32[]{:S(2)}) copy-start(bf16[2048,512]{1,0:T(8,128)(2,1)} %param.17) | copy-start | bytes 6291460
  368.5 12.4 %copy-start.11 = (f32[2048]{0:T(1024)S(1)}, f32[2048]{0:T(1024)}, u32[]{:S(2)}) copy-start(f32[2048]{0:T(1024)} %param.16) | copy-start | bytes 24580
  368.5 13.6 %copy-start.1 = (bf16[1,1,704,2048]{3,2,1,0:T(8,128)(2,1)S(1)}, bf16[1,1,704,2048]{3,2,1,0:T(8,128)(2,1)}, u32[]{:S(2)}) copy-start(bf16[1,1,704,2048]{3,2,1,0:T(8,128)(2,1)} %param.15) | copy-start | bytes 8650756
  380.9 1.2 copy-start.7
Sparse Core Ops, SparseCore 0:
  11.4 118.0 all-gather.1

commit v2 on v1

--- a/solution.py
+++ b/solution.py
@@ -155,18 +155,14 @@
 
 
 GROUP = 512
+CHUNKS = 2
+PARTS = 3
+LANES = 128
 
 
 def exchanged(value, axis, mask):
     pairs = [(source, source ^ mask) for source in range(lax.axis_size(axis))]
-    return lax.ppermute(value, axis, pairs)
-
-
-def halve(value, dim, bit, axis, mask):
-    kept = lax.dynamic_index_in_dim(value, bit, dim, keepdims=False)
-    sent = lax.dynamic_index_in_dim(value, 1 - bit, dim, keepdims=False)
-    came = exchanged(sent.astype(jnp.bfloat16), axis, mask)
-    return kept.astype(jnp.float32) + came.astype(jnp.float32)
+    return lax.ppermute(value.astype(jnp.bfloat16), axis, pairs)
 
 
 def gate_table(normed, router_weight, expert_ids):
@@ -177,6 +173,20 @@
     affinity = jnp.where(choose, jax.nn.sigmoid(logits), 0.0)
     share = affinity / jnp.sum(affinity, axis=1, keepdims=True)
     return jnp.where(choose, share, -1.0)
+
+
+def in_parts(table):
+    parts, rest = [], table
+    for _ in range(PARTS):
+        part = lax.reduce_precision(rest, 8, 7)
+        parts.append(part.astype(jnp.bfloat16))
+        rest = rest - part
+    pad = LANES - PARTS * table.shape[1]
+    return jnp.pad(jnp.concatenate(parts, axis=1), ((0, 0), (0, pad)))
+
+
+def flipped_if(value, bit, dim):
+    return jnp.where(bit == 1, jnp.flip(value, dim), value)
 
 
 def gather_body(
@@ -193,6 +203,7 @@
     segment = lax.axis_index("segment")
     column = lax.axis_index("exp")
     columns = lax.axis_size("exp")
+    segments = lax.axis_size("segment")
     half_index = segment % 2
     expert = (segment // 2) * columns + column
     core, along_x, along_y = column % 2, (column // 2) % 2, column // 4
@@ -201,73 +212,107 @@
     experts = router_weight.shape[1]
     capacity = GROUP * expert_ids.shape[1] * 5 // (4 * experts)
     w_gate, w_up, w_down = gate_weight[0, 0], up_weight[0, 0], down_weight[0, 0]
-    half_units = w_gate.shape[0]
+    chunk_rows = tok_rows // CHUNKS
+    tokens = segments * columns * chunk_rows
+    groups = tokens // GROUP
 
     residual = hidden_rows.astype(jnp.float32)
     normed = rms_norm(residual, norm_gain).astype(jnp.bfloat16)
-    table = gate_table(normed, router_weight, expert_ids)
-    everywhere = ("segment", "exp")
-    all_table = lax.all_gather(table, everywhere, axis=0, tiled=True)
-    all_rows = lax.all_gather(normed, everywhere, axis=0, tiled=True)
-
-    own = jnp.arange(experts, dtype=jnp.int32) == expert
-    gates = jnp.sum(jnp.where(own[None, :], all_table, 0.0), axis=1).reshape(-1, GROUP)
-    named = gates >= 0.0
-    count = jnp.sum(named.astype(jnp.float32))
+    table = in_parts(gate_table(normed, router_weight, expert_ids))
+    packed = jnp.concatenate([normed, table], axis=1)
+    gathered = [
+        lax.all_gather(
+            packed[chunk * chunk_rows : (chunk + 1) * chunk_rows],
+            ("segment", "exp"),
+            axis=0,
+            tiled=True,
+        )
+        for chunk in range(CHUNKS)
+    ]
+
+    lane = jnp.arange(LANES, dtype=jnp.int32)
+    own_lane = (lane % experts == expert) & (lane < PARTS * experts)
     place = jnp.arange(GROUP, dtype=jnp.int32)
     earlier = (place[:, None] < place[None, :]).astype(jnp.bfloat16)
-    rank = jnp.dot(named.astype(jnp.bfloat16), earlier, preferred_element_type=jnp.float32)
-    rank = jnp.where(named, rank.astype(jnp.int32), -1)
     slots = jnp.arange(capacity, dtype=jnp.int32)
-    picks = rank[:, None, :] == slots[None, :, None]
-    slot_gates = jnp.sum(jnp.where(picks, gates[:, None, :], 0.0), axis=2)
-    picks = picks.astype(jnp.bfloat16)
-    groups = picks.shape[0]
-
-    rows = lax.dot_general(
-        picks,
-        all_rows.reshape(groups, GROUP, model_width),
-        (((2,), (1,)), ((0,), (0,))),
-        preferred_element_type=jnp.float32,
-    ).astype(jnp.bfloat16)
-    rows = rows.reshape(groups * capacity, model_width)
     by_units = (((1,), (1,)), ((), ()))
-    gate_pre = lax.dot_general(rows, w_gate, by_units, preferred_element_type=jnp.float32)
-    up_pre = lax.dot_general(rows, w_up, by_units, preferred_element_type=jnp.float32)
-    hidden = (jax.nn.silu(gate_pre) * up_pre).astype(jnp.bfloat16)
-    other_hidden = exchanged(hidden, "segment", 1)
-    out = jnp.dot(hidden, w_down, preferred_element_type=jnp.float32)
-    out = (out * slot_gates.reshape(-1, 1)).astype(jnp.bfloat16)
-    mix = lax.dot_general(
-        picks,
-        out.reshape(groups, capacity, model_width),
-        (((1,), (1,)), ((0,), (0,))),
-        preferred_element_type=jnp.float32,
-    ).astype(jnp.bfloat16)
-    mix = mix.reshape(2, 2, 2, 2, 2, tok_rows, model_width)
-    mix = halve(mix, 4, core, "exp", 1)
-    first = halve(mix[..., :width_half], 3, along_x, "exp", 2)
-    second = halve(mix[..., width_half:], 2, along_y, "exp", 4)
-    first = halve(first, 2, along_y, "exp", 4)
-    second = halve(second, 2, along_x, "exp", 2)
-    mix = jnp.concatenate([first, second], axis=-1)
-    mix = halve(mix, 0, segment // 2, "segment", 2)
-    mix = halve(mix, 0, segment % 2, "segment", 1)
-
-    expert_mix = mix.astype(jnp.bfloat16)
+    by_slots = (((0,), (0,)), ((), ()))
+    count = jnp.zeros((), jnp.float32)
+    all_received, all_hidden, all_other, mixes = [], [], [], []
+    for chunk in range(CHUNKS):
+        if chunk:
+            gathered[chunk], _ = lax.optimization_barrier((gathered[chunk], sent))
+        tail = gathered[chunk][:, model_width:].astype(jnp.float32)
+        gates = jnp.sum(jnp.where(own_lane[None, :], tail, 0.0), axis=1).reshape(groups, GROUP)
+        named = gates >= 0.0
+        count = count + jnp.sum(named.astype(jnp.float32))
+        rank = jnp.dot(named.astype(jnp.bfloat16), earlier, preferred_element_type=jnp.float32)
+        rank = jnp.where(named, rank.astype(jnp.int32), -1)
+        picks = rank[:, None, :] == slots[None, :, None]
+        slot_gates = jnp.sum(jnp.where(picks, gates[:, None, :], 0.0), axis=2)
+        received = lax.dot_general(
+            picks.astype(jnp.bfloat16),
+            gathered[chunk][:, :model_width].reshape(groups, GROUP, model_width),
+            (((2,), (1,)), ((0,), (0,))),
+            preferred_element_type=jnp.float32,
+        ).astype(jnp.bfloat16)
+        received = received.reshape(groups * capacity, model_width)
+        gate_pre = lax.dot_general(received, w_gate, by_units, preferred_element_type=jnp.float32)
+        up_pre = lax.dot_general(received, w_up, by_units, preferred_element_type=jnp.float32)
+        hidden = (jax.nn.silu(gate_pre) * up_pre).astype(jnp.bfloat16)
+        all_received.append(received)
+        all_hidden.append(hidden)
+        all_other.append(exchanged(hidden, "segment", 1))
+        out = jnp.dot(hidden, w_down, preferred_element_type=jnp.float32)
+        out = (out * slot_gates.reshape(-1, 1)).astype(jnp.bfloat16)
+        out = out.reshape(groups, capacity, model_width)
+
+        near = rank.reshape(groups, 2, 2, 2, chunk_rows)
+        near = flipped_if(flipped_if(flipped_if(near, core, 3), along_x, 2), along_y, 1)
+
+        def scattered(places):
+            hits = (places.reshape(groups, 1, -1) == slots[None, :, None]).astype(jnp.bfloat16)
+            return lax.dot_general(
+                hits, out, (((1,), (1,)), ((0,), (0,))), preferred_element_type=jnp.float32
+            ).reshape(groups, 2, 2, chunk_rows, model_width)
+
+        sent = scattered(near[:, :, :, 1]).astype(jnp.bfloat16)
+        came = exchanged(sent, "exp", 1)
+        mix = scattered(near[:, :, :, 0]) + came.astype(jnp.float32)
+        first, second = mix[..., :width_half], mix[..., width_half:]
+        first_came = exchanged(first[:, :, 1], "exp", 2)
+        second_came = exchanged(second[:, 1], "exp", 4)
+        first = first[:, :, 0] + first_came.astype(jnp.float32)
+        second = second[:, 0] + second_came.astype(jnp.float32)
+        first_came = exchanged(first[:, 1], "exp", 4)
+        second_came = exchanged(second[:, 1], "exp", 2)
+        first = first[:, 0] + first_came.astype(jnp.float32)
+        second = second[:, 0] + second_came.astype(jnp.float32)
+        mix = jnp.concatenate([first, second], axis=-1)
+        mix = flipped_if(mix.reshape(2, 2, chunk_rows, model_width), segment // 2, 0)
+        mix = mix[0] + exchanged(mix[1], "segment", 2).astype(jnp.float32)
+        mix = flipped_if(mix, segment % 2, 0)
+        mixes.append(mix[0] + exchanged(mix[1], "segment", 1).astype(jnp.float32))
+
+    expert_mix = jnp.concatenate(mixes, axis=0).astype(jnp.bfloat16)
     combined = residual + expert_mix.astype(jnp.float32)
     normed_next = rms_norm(combined, latent_gain).astype(jnp.bfloat16)
     latents = jnp.dot(normed_next, kv_weight, preferred_element_type=jnp.float32).astype(
         jnp.bfloat16
     )
-    by_slots = (((0,), (0,)), ((), ()))
+    gram_in, gram_hid = 0.0, 0.0
+    for received, hidden, other_hidden in zip(all_received, all_hidden, all_other):
+        own_columns = lax.dynamic_slice_in_dim(received, half_index * width_half, width_half, 1)
+        gram_in = gram_in + lax.dot_general(
+            own_columns, received, by_slots, preferred_element_type=jnp.float32
+        )
+        first_half = jnp.where(half_index == 0, hidden, other_hidden)
+        second_half = jnp.where(half_index == 0, other_hidden, hidden)
+        full_hidden = jnp.concatenate([first_half, second_half], axis=1)
+        gram_hid = gram_hid + lax.dot_general(
+            hidden, full_hidden, by_slots, preferred_element_type=jnp.float32
+        )
     inverse_count = 2.0 / count
-    own_columns = lax.dynamic_slice_in_dim(rows, half_index * width_half, width_half, 1)
-    gram_in = lax.dot_general(own_columns, rows, by_slots, preferred_element_type=jnp.float32)
-    first_half = jnp.where(half_index == 0, hidden, other_hidden)
-    second_half = jnp.where(half_index == 0, other_hidden, hidden)
-    full_hidden = jnp.concatenate([first_half, second_half], axis=1)
-    gram_hid = lax.dot_general(hidden, full_hidden, by_slots, preferred_element_type=jnp.float32)
     return (
         expert_mix,
         latents,

time: 389 us -> 412 us (1.059); the launches traced: 389 us -> 406 us
  blocking collectives: 44.9 us -> 0 us
  waiting for transfers between devices: 192 us -> 224 us
  matrix products: 66.9 us -> 84.9 us
  starting transfers between devices: 7.01 us -> 15.4 us
  other arithmetic: 27 us -> 35 us
  local copies, waits for them, and re-layouts: 36.1 us -> 29.8 us
    all_gather x1 -> x2, waiting for transfers between devices: 71 us -> 129 us  [gather_body(): lax.all_gather(packed[chunk * chunk_rows:(chunk + 1) * chunk_rows], ('seg...]
    all_gather x1 -> x0, blocking collectives: 44.9 us -> none  [gather_body(): all_table = lax.all_gather(table, everywhere, axis=0, tiled=True)]
    ppermute x8 -> x16, waiting for transfers between devices: 121 us -> 94.9 us  [exchanged(): return lax.ppermute(value.astype(jnp.bfloat16), axis, pairs)]
    dynamic_slice x2 -> x0, local copies, waits for them, and re-layouts: 20.3 us -> none  [the longest x1 12 us: halve(): kept = lax.dynamic_index_in_dim(value, bit, dim, keepdims=False)]
    dot_general x5 -> x12, matrix products: 47.4 us -> 62.9 us  [the longest x2 20.1 us: gather_body(): lax.dot_general(own_columns, received, by_slots, preferred_element_type=j...]
    slice x1 -> x5, local copies, waits for them, and re-layouts: 6.76 us -> 17.8 us  [the longest x2 16.9 us: gather_body(): gathered[chunk][:, :model_width].reshape(groups, GROUP, model_width)]
    ppermute x8 -> x16, starting transfers between devices: 6.97 us -> 15.3 us  [exchanged(): return lax.ppermute(value.astype(jnp.bfloat16), axis, pairs)]
    add x6 -> x12, other arithmetic: 18.8 us -> 22.7 us  [the longest x2 16.9 us: gather_body(): mix = scattered(near[:, :, :, 0]) + came.astype(jnp.float32)]
  transfers between devices with their start and end apart: 9 -> 18, of which waited for: 8 -> 12; matrix products, arithmetic and copies ran while one was open for 12% -> 32% of each run, Pallas kernels for 0% -> 0%
where the time goes in v2:
time: 412 us; the launch traced here: 406 us
  waiting for transfers between devices  224 us (54%)
  matrix products  84.9 us (21%)
  other arithmetic  35 us (8%)
  local copies, waits for them, and re-layouts  29.8 us (7%)
  between operations  16.3 us (4%)
  starting transfers between devices  15.4 us (4%)
    all_gather x2, waiting for transfers between devices, gather_body(): lax.all_gather(packed[chunk * chunk_rows:(chunk + 1) * chunk_rows], ('seg...  129 us
    ppermute x16, waiting for transfers between devices, exchanged(): return lax.ppermute(value.astype(jnp.bfloat16), axis, pairs)  94.9 us
    dot_general x2, matrix products, gather_body(): lax.dot_general(own_columns, received, by_slots, preferred_element_type=j...  20.1 us
    add x2, other arithmetic, gather_body(): mix = scattered(near[:, :, :, 0]) + came.astype(jnp.float32)  16.9 us
    slice x2, local copies, waits for them, and re-layouts, gather_body(): gathered[chunk][:, :model_width].reshape(groups, GROUP, model_width)  16.9 us
    ppermute x16, starting transfers between devices, exchanged(): return lax.ppermute(value.astype(jnp.bfloat16), axis, pairs)  15.3 us
    dot_general x4, matrix products, scattered(): lax.dot_general(hits, out, (((1,), (1,)), ((0,), (0,))), preferred_elemen...  14.9 us
    dot_general x2, matrix products, gather_body(): lax.dot_general(picks.astype(jnp.bfloat16), gathered[chunk][:, :model_wid...  11.5 us
  transfers between devices with their start and end apart: 18, of which 12 were waited for; matrix products, arithmetic and copies ran while one was open for 32% of the time, Pallas kernels for 0%

profile of v2, /device:TPU:0, one launch (start us, length us, event | category | flops | bytes accessed | tf_op | source)
XLA Modules:
  0.0 405.5 jit_solution(2677544311092487026)
XLA Ops:
  7.2 1.4 fusion.35
  8.6 0.7 fusion.67
  9.3 1.2 fusion.37
  10.6 1.1 fusion.81
  11.9 0.8 fusion.80
  12.8 0.7 all-gather.5.cloned.1.call-update
  13.6 81.6 %all-gather.3.cloned.1.call-done = bf16[2048,2176]{1,0:T(8,128)(2,1)} async-done(((bf16[64,2176]{1,0:T(8,128)(2,1)}), bf16[2048,2176]{1,0:T(8,128)(2,1)}) %all-gather.3.cloned.1.call-update) | async-done | bytes 8912912 | tf_op jit(solution)/shard_map/all_gather | solution.py:224
  95.2 1.3 select_reduce_fusion.3
  97.3 8.4 %slice.163 = bf16[2048,2048]{1,0:T(8,128)(2,1)} slice(bf16[2048,2176]{1,0:T(8,128)(2,1)} %all-gather.3.cloned.1.call-done), slice={[0:2048], [0:2048]} | slice | bytes 16777216 | tf_op jit(solution)/shard_map/slice | solution.py:255
  105.8 5.8 %convolution_convert_fusion.3 = bf16[4,240,2048]{2,1,0:T(8,128)(2,1)S(1)} fusion(bf16[4,512,2048]{2,1,0:T(8,128)(2,1)} %bitcast.137, s32[4,512]{1,0:T(4,128)S(1)} %fusion.30), kind=kOutput, calls=%fused_computation.9 | convolution fusion | flops 2015723520 | bytes 12328960 | tf_op jit(solution)/shard_map/dot_general | solution.py:253
  111.6 3.2 fusion.11
  114.8 4.9 %multiply_convert_fusion.3 = bf16[960,704]{0,1:T(8,128)(2,1)} fusion(f32[960,704]{0,1:T(8,128)S(1)} %fusion.11, bf16[960,2048]{1,0:T(8,128)(2,1)S(1)} %bitcast.148, bf16[1,1,704,2048]{3,2,1,0:T(8,128)(2,1)S(1)} %copy-done.12), kind=kOutput, calls=%fused_computation.30 | convolution fusion | flops 2772295680 | bytes 10870784 | tf_op jit(solution)/shard_map/dot_general | solution.py:260
  119.7 4.9 %multiply_convert_fusion.1 = bf16[960,2048]{1,0:T(8,128)(2,1)S(1)} fusion(bf16[960,704]{0,1:T(8,128)(2,1)} %multiply_convert_fusion.3, f32[960]{0:T(1024)S(1)} %mul.98, bf16[1,1,704,2048]{3,2,1,0:T(8,128)(2,1)S(1)} %copy-done), kind=kOutput, calls=%fused_computation.4 | convolution fusion | flops 2772172800 | bytes 8171264 | tf_op jit(solution)/shard_map/dot_general | solution.py:266
  124.6 1.9 copy-done.2
  126.5 3.3 convolution_convert_fusion.1
  129.8 47.0 %all-gather.5.cloned.1.call-done = bf16[2048,2176]{1,0:T(8,128)(2,1)} async-done(((bf16[64,2176]{1,0:T(8,128)(2,1)}), bf16[2048,2176]{1,0:T(8,128)(2,1)}) %all-gather.5.cloned.1.call-update) | async-done | bytes 8912912 | tf_op jit(solution)/shard_map/all_gather | solution.py:224
  176.8 8.4 %slice.146 = bf16[2048,2048]{1,0:T(8,128)(2,1)} slice(bf16[2048,2176]{1,0:T(8,128)(2,1)} %all-gather.5.cloned.1.call-done), slice={[0:2048], [0:2048]} | slice | bytes 16777216 | tf_op jit(solution)/shard_map/slice | solution.py:255
  185.3 1.3 select_reduce_fusion.2
  186.5 1.6 collective-permute-start.14
  188.7 5.7 %convolution_convert_fusion.2 = bf16[4,240,2048]{2,1,0:T(8,128)(2,1)S(1)} fusion(bf16[4,512,2048]{2,1,0:T(8,128)(2,1)} %bitcast.136, s32[4,512]{1,0:T(4,128)S(1)} %fusion.29), kind=kOutput, calls=%fused_computation.8 | convolution fusion | flops 2015723520 | bytes 12328960 | tf_op jit(solution)/shard_map/dot_general | solution.py:253
  194.5 3.2 fusion.9
  197.7 5.1 %multiply_convert_fusion.2 = bf16[960,704]{0,1:T(8,128)(2,1)} fusion(f32[960,704]{0,1:T(8,128)S(1)} %fusion.9, bf16[960,2048]{1,0:T(8,128)(2,1)S(1)} %bitcast.151, bf16[1,1,704,2048]{3,2,1,0:T(8,128)(2,1)S(1)} %copy-done.13), kind=kOutput, calls=%fused_computation.29 | convolution fusion | flops 2772295680 | bytes 10870784 | tf_op jit(solution)/shard_map/dot_general | solution.py:260
  203.6 4.9 %multiply_convert_fusion = bf16[960,2048]{1,0:T(8,128)(2,1)S(1)} fusion(bf16[960,704]{0,1:T(8,128)(2,1)} %multiply_convert_fusion.2, f32[960]{0:T(1024)S(1)} %mul.103, bf16[1,1,704,2048]{3,2,1,0:T(8,128)(2,1)S(1)} %copy-done), kind=kOutput, calls=%fused_computation.3 | convolution fusion | flops 2772172800 | bytes 8171264 | tf_op jit(solution)/shard_map/dot_general | solution.py:266
  208.6 3.4 convolution_convert_fusion
  212.0 0.7 copy-done.3
  212.9 0.7 copy-done.7
  213.6 7.0 %fusion.26 = f32[1024,2048]{1,0:T(8,128)} fusion(bf16[960,2048]{1,0:T(8,128)(2,1)S(1)} %bitcast.149, s32[]{:T(128)S(6)} %select_n.179), kind=kOutput, calls=%fused_computation.42 | convolution fusion | flops 4026531840 | bytes 14286852 | tf_op jit(solution)/shard_map/dot_general | solution.py:306
  220.6 0.6 convert_reduce_fusion
  222.5 13.1 %multiply_bitcast_fusion = f32[1,1,1024,2048]{3,2,1,0:T(8,128)} fusion(f32[1024,2048]{1,0:T(8,128)} %fusion.26, f32[]{:T(128)S(6)} %div.67, bf16[960,2048]{1,0:T(8,128)(2,1)} %bitcast.152, s32[]{:T(128)S(6)} %select_n.179), kind=kOutput, calls=%fused_computation | convolution fusion | flops 4030726144 | bytes 22675464 | tf_op jit(solution)/shard_map/dot_general | solution.py:306
  235.8 6.9 %fusion.46 = f32[4,256,2048]{2,1,0:T(8,128)} fusion(bf16[4,240,2048]{2,1,0:T(8,128)(2,1)} %bitcast.141, s32[4,256]{1,0:T(4,128)S(1)} %eq.153), kind=kOutput, calls=%fused_computation.105 | convolution fusion | flops 1006878720 | bytes 12324864 | tf_op jit(solution)/shard_map/dot_general | solution.py:275
  242.7 1.3 fusion.47
  244.0 7.6 %collective-permute-done.15 = bf16[960,704]{0,1:T(8,128)(2,1)} collective-permute-done((bf16[960,704]{0,1:T(8,128)(2,1)}, bf16[960,704]{0,1:T(8,128)(2,1)}, u32[]{:S(2)}, u32[]{:S(2)}) %collective-permute-start.15) | collective-permute-done | bytes 1351712 | tf_op jit(solution)/shard_map/ppermute | solution.py:165
  251.6 2.0 broadcast_select_fusion.1
  253.6 2.0 broadcast_select_fusion.3
  255.6 3.8 fusion.3
  259.4 5.8 %multiply_bitcast_fusion.1 = f32[1,1,704,1408]{3,2,1,0:T(8,128)} fusion(f32[704,1408]{1,0:T(8,128)S(1)} %fusion.3, bf16[960,704]{0,1:T(8,128)(2,1)} %multiply_convert_fusion.3, bf16[960,704]{0,1:T(8,128)(2,1)S(1)} %get-tuple-element.13, bf16[960,704]{0,1:T(8,128)(2,1)S(1)} %get-tuple-element.12, f32[]{:T(128)S(6)} %div.67), kind=kOutput, calls=%fused_computation.5 | convolution fusion | flops 1910554624 | bytes 11984900 | tf_op jit(solution)/shard_map/dot_general | solution.py:312
  265.2 10.2 %convert_add_fusion.1 = f32[4,2,2,64,2048]{4,3,2,1,0:T(8,128)} fusion(f32[4,2,2,64,2048]{4,3,2,1,0:T(8,128)} %bitcast.135, bf16[4,2,2,64,2048]{4,3,2,1,0:T(8,128)(2,1)} %collective-permute-done), kind=kLoop, calls=%fused_computation.2 | loop fusion | flops 4194304 | bytes 20971520 | tf_op jit(solution)/shard_map/add | solution.py:281
  275.4 1.8 slice_bitcast_fusion.13
  277.1 1.3 collective-permute-start.1
  278.5 1.8 slice_bitcast_fusion.11
  280.2 0.8 collective-permute-start.3
  281.1 6.7 %convert_add_fusion = f32[4,2,2,64,2048]{4,3,2,1,0:T(8,128)} fusion(f32[4,2,2,64,2048]{4,3,2,1,0:T(8,128)S(1)} %bitcast.134, bf16[4,2,2,64,2048]{4,3,2,1,0:T(8,128)(2,1)} %collective-permute-done.7), kind=kLoop, calls=%fused_computation.1 | loop fusion | flops 4194304 | bytes 20971520 | tf_op jit(solution)/shard_map/add | solution.py:281
  287.8 1.9 slice_bitcast_fusion.8
  289.7 1.5 collective-permute-start.8
  291.2 1.7 slice_bitcast_fusion.6
  293.0 0.6 collective-permute-start.10
  293.6 9.7 %collective-permute-done.1 = bf16[4,2,64,1024]{3,2,0,1:T(8,128)(2,1)S(1)} collective-permute-done((bf16[4,2,64,1024]{3,2,0,1:T(8,128)(2,1)S(1)}, bf16[4,2,64,1024]{3,2,0,1:T(8,128)(2,1)S(1)}, u32[]{:S(2)}, u32[]{:S(2)}) %collective-permute-start.1) | collective-permute-done | bytes 1048608 | tf_op jit(solution)/shard_map/ppermute | solution.py:165
  303.3 2.0 fusion.20
  305.4 1.5 collective-permute-start.2
  307.0 1.9 fusion.19
  309.0 0.6 collective-permute-start.4
  309.6 16.2 %collective-permute-done.8 = bf16[4,2,64,1024]{3,2,0,1:T(8,128)(2,1)S(1)} collective-permute-done((bf16[4,2,64,1024]{3,2,0,1:T(8,128)(2,1)S(1)}, bf16[4,2,64,1024]{3,2,0,1:T(8,128)(2,1)S(1)}, u32[]{:S(2)}, u32[]{:S(2)}) %collective-permute-start.8) | collective-permute-done | bytes 1048608 | tf_op jit(solution)/shard_map/ppermute | solution.py:165
  326.3 1.5 collective-permute-start.9
  327.9 1.0 collective-permute-done.10
  329.4 0.8 collective-permute-start.11
  330.2 9.9 %collective-permute-done.2 = bf16[4,64,1024]{2,1,0:T(8,128)(2,1)S(1)} collective-permute-done((bf16[4,64,1024]{2,1,0:T(8,128)(2,1)S(1)}, bf16[4,64,1024]{2,1,0:T(8,128)(2,1)S(1)}, u32[]{:S(2)}, u32[]{:S(2)}) %collective-permute-start.2) | collective-permute-done | bytes 524320 | tf_op jit(solution)/shard_map/ppermute | solution.py:165
  340.8 2.0 collective-permute-start.5
  342.8 6.7 %collective-permute-done.9 = bf16[4,64,1024]{2,1,0:T(8,128)(2,1)S(1)} collective-permute-done((bf16[4,64,1024]{2,1,0:T(8,128)(2,1)S(1)}, bf16[4,64,1024]{2,1,0:T(8,128)(2,1)S(1)}, u32[]{:S(2)}, u32[]{:S(2)}) %collective-permute-start.9) | collective-permute-done | bytes 524320 | tf_op jit(solution)/shard_map/ppermute | solution.py:165
  350.2 2.0 collective-permute-start.12
  352.2 23.3 %collective-permute-done.5 = bf16[2,64,2048]{2,1,0:T(8,128)(2,1)S(1)} collective-permute-done((bf16[2,64,2048]{2,1,0:T(8,128)(2,1)S(1)}, bf16[2,64,2048]{2,1,0:T(8,128)(2,1)S(1)}, u32[]{:S(2)}, u32[]{:S(2)}) %collective-permute-start.5) | collective-permute-done | bytes 524320 | tf_op jit(solution)/shard_map/ppermute | solution.py:165
  375.9 9.9 %collective-permute-done.12 = bf16[2,64,2048]{2,1,0:T(8,128)(2,1)S(1)} collective-permute-done((bf16[2,64,2048]{2,1,0:T(8,128)(2,1)S(1)}, bf16[2,64,2048]{2,1,0:T(8,128)(2,1)S(1)}, u32[]{:S(2)}, u32[]{:S(2)}) %collective-permute-start.12) | collective-permute-done | bytes 524320 | tf_op jit(solution)/shard_map/ppermute | solution.py:165
  386.2 5.2 %collective-permute-done.6 = bf16[64,2048]{1,0:T(8,128)(2,1)S(1)} collective-permute-done((bf16[64,2048]{1,0:T(8,128)(2,1)S(1)}, bf16[64,2048]{1,0:T(8,128)(2,1)S(1)}, u32[]{:S(2)}, u32[]{:S(2)}) %collective-permute-start.6) | collective-permute-done | bytes 262176 | tf_op jit(solution)/shard_map/ppermute | solution.py:165
  391.5 5.5 %collective-permute-done.13 = bf16[64,2048]{1,0:T(8,128)(2,1)S(1)} collective-permute-done((bf16[64,2048]{1,0:T(8,128)(2,1)S(1)}, bf16[64,2048]{1,0:T(8,128)(2,1)S(1)}, u32[]{:S(2)}, u32[]{:S(2)}) %collective-permute-start.13) | collective-permute-done | bytes 262176 | tf_op jit(solution)/shard_map/ppermute | solution.py:165
  397.3 1.1 convolution_convert_fusion.4
  (104 shorter events, 6.7 us)
Async XLA Ops:
  7.2 112.6 %copy-start = (bf16[1,1,704,2048]{3,2,1,0:T(8,128)(2,1)S(1)}, bf16[1,1,704,2048]{3,2,1,0:T(8,128)(2,1)}, u32[]{:S(2)}) copy-start(bf16[1,1,704,2048]{3,2,1,0:T(8,128)(2,1)} %param.15) | copy-start | bytes 8650756
  7.2 88.0 %all-gather.3.cloned.1.call-start = ((), (), s32[]{:S(2)}) async-start(), calls=%async_computation | async-start | bytes 9191424 | tf_op jit(solution)/shard_map/all_gather | solution.py:224
  12.8 164.1 %all-gather.5.cloned.1.call-start = ((), (), s32[]{:S(2)}) async-start(), calls=%async_computation.1 | async-start | bytes 9191424 | tf_op jit(solution)/shard_map/all_gather | solution.py:224
  105.8 5.8 %copy-start.10 = (bf16[1,1,704,2048]{3,2,1,0:T(8,128)(2,1)S(1)}, bf16[1,1,704,2048]{3,2,1,0:T(8,128)(2,1)}, u32[]{:S(2)}) copy-start(bf16[1,1,704,2048]{3,2,1,0:T(8,128)(2,1)} %param.14) | copy-start | bytes 8650756
  111.6 3.2 copy-start.6
  111.6 3.2 copy-start.12
  124.6 1.9 copy-start.2
  186.5 67.0 %collective-permute-start.14 = (bf16[960,704]{0,1:T(8,128)(2,1)}, bf16[960,704]{0,1:T(8,128)(2,1)}, u32[]{:S(2)}, u32[]{:S(2)}) collective-permute-start(bf16[960,704]{0,1:T(8,128)(2,1)} %multiply_convert_fusion.3), channel_id=1, source_target_pairs={{0,8},{8,0},{16,24},{24,16},{1,9},{9,1},{17,25},{25,17},{2,10},{10... | collective-permute-start | bytes 4055048 | tf_op jit(solution)/shard_map/ppermute | solution.py:165
  188.1 77.0 %collective-permute-start = (bf16[4,2,2,64,2048]{4,3,2,1,0:T(8,128)(2,1)}, bf16[4,2,2,64,2048]{4,3,2,1,0:T(8,128)(2,1)}, u32[]{:S(2)}, u32[]{:S(2)}) collective-permute-start(bf16[4,2,2,64,2048]{4,3,2,1,0:T(8,128)(2,1)} %bitcast.144), channel_id=1, source_target_pairs={{0,1},{1,0},{2,3},{3,2},{4,5},{5,4},{6,7},{7,6},{8,9},{9,8},{10,11... | collective-permute-start | bytes 12582920 | tf_op jit(solution)/shard_map/ppermute | solution.py:165
  188.7 5.8 %copy-start.11 = (bf16[1,1,704,2048]{3,2,1,0:T(8,128)(2,1)S(1)}, bf16[1,1,704,2048]{3,2,1,0:T(8,128)(2,1)}, u32[]{:S(2)}) copy-start(bf16[1,1,704,2048]{3,2,1,0:T(8,128)(2,1)} %param.14) | copy-start | bytes 8650756
  194.5 3.2 copy-start.8
  194.5 3.2 copy-start.13
  202.8 48.8 %collective-permute-start.15 = (bf16[960,704]{0,1:T(8,128)(2,1)}, bf16[960,704]{0,1:T(8,128)(2,1)}, u32[]{:S(2)}, u32[]{:S(2)}) collective-permute-start(bf16[960,704]{0,1:T(8,128)(2,1)} %multiply_convert_fusion.2), channel_id=1, source_target_pairs={{0,8},{8,0},{16,24},{24,16},{1,9},{9,1},{17,25},{25,17},{2,10},{10... | collective-permute-start | bytes 4055048 | tf_op jit(solution)/shard_map/ppermute | solution.py:165
  208.5 4.1 %copy-start.3 = (bf16[960,2048]{1,0:T(8,128)(2,1)}, bf16[960,2048]{1,0:T(8,128)(2,1)S(1)}, u32[]{:S(2)}) copy-start(bf16[960,2048]{1,0:T(8,128)(2,1)S(1)} %multiply_convert_fusion) | copy-start | bytes 11796484
  208.5 5.0 %copy-start.7 = (bf16[4,240,2048]{2,1,0:T(8,128)(2,1)S(1)}, bf16[4,240,2048]{2,1,0:T(8,128)(2,1)}, u32[]{:S(2)}) copy-start(bf16[4,240,2048]{2,1,0:T(8,128)(2,1)} %copy-done.6) | copy-start | bytes 11796484
  212.7 68.4 %collective-permute-start.7 = (bf16[4,2,2,64,2048]{4,3,2,1,0:T(8,128)(2,1)}, bf16[4,2,2,64,2048]{4,3,2,1,0:T(8,128)(2,1)}, u32[]{:S(2)}, u32[]{:S(2)}) collective-permute-start(bf16[4,2,2,64,2048]{4,3,2,1,0:T(8,128)(2,1)} %bitcast.25), channel_id=1, source_target_pairs={{0,1},{1,0},{2,3},{3,2},{4,5},{5,4},{6,7},{7,6},{8,9},{9,8},{10,11... | collective-permute-start | bytes 12582920 | tf_op jit(solution)/shard_map/ppermute | solution.py:165
  235.8 6.9 %copy-start.4 = (bf16[960,2048]{1,0:T(8,128)(2,1)S(1)}, bf16[960,2048]{1,0:T(8,128)(2,1)}, u32[]{:S(2)}) copy-start(bf16[960,2048]{1,0:T(8,128)(2,1)} %copy-done.3) | copy-start | bytes 11796484
  277.1 26.2 %collective-permute-start.1 = (bf16[4,2,64,1024]{3,2,0,1:T(8,128)(2,1)S(1)}, bf16[4,2,64,1024]{3,2,0,1:T(8,128)(2,1)S(1)}, u32[]{:S(2)}, u32[]{:S(2)}) collective-permute-start(bf16[4,2,64,1024]{3,2,0,1:T(8,128)(2,1)S(1)} %slice_bitcast_fusion.13), channel_id=1, source_target_pairs={{0,2},{1,3},{2,0},{3,1},{4,6},{5,7},{6,4},{7,5},{8,10},{9,11},{10,... | collective-permute-start | bytes 3145736 | tf_op jit(solution)/shard_map/ppermute | solution.py:165
  280.2 26.8 %collective-permute-start.3 = (bf16[4,2,64,1024]{3,2,0,1:T(8,128)(2,1)S(1)}, bf16[4,2,64,1024]{3,2,0,1:T(8,128)(2,1)S(1)}, u32[]{:S(2)}, u32[]{:S(2)}) collective-permute-start(bf16[4,2,64,1024]{3,2,0,1:T(8,128)(2,1)S(1)} %slice_bitcast_fusion.11), channel_id=1, source_target_pairs={{0,4},{1,5},{2,6},{3,7},{4,0},{5,1},{6,2},{7,3},{8,12},{9,13},{10,... | collective-permute-start | bytes 3145736 | tf_op jit(solution)/shard_map/ppermute | solution.py:165
  287.8 38.0 %slice-start = ((s8[8388608]{0:T(1024)(128)(4,1)}), s8[4194304]{0:T(1024)(128)(4,1)S(1)}, s32[]{:S(2)}) async-start(s8[8388608]{0:T(1024)(128)(4,1)} %bitcast.138), calls=%async_computation.2 | async-start | bytes 8388608
  289.7 36.1 %collective-permute-start.8 = (bf16[4,2,64,1024]{3,2,0,1:T(8,128)(2,1)S(1)}, bf16[4,2,64,1024]{3,2,0,1:T(8,128)(2,1)S(1)}, u32[]{:S(2)}, u32[]{:S(2)}) collective-permute-start(bf16[4,2,64,1024]{3,2,0,1:T(8,128)(2,1)S(1)} %slice_bitcast_fusion.8), channel_id=1, source_target_pairs={{0,2},{1,3},{2,0},{3,1},{4,6},{5,7},{6,4},{7,5},{8,10},{9,11},{10,... | collective-permute-start | bytes 3145736 | tf_op jit(solution)/shard_map/ppermute | solution.py:165
  293.0 32.8 %slice-start.1 = ((s8[8388608]{0:T(1024)(128)(4,1)}), s8[4194304]{0:T(1024)(128)(4,1)S(1)}, s32[]{:S(2)}) async-start(s8[8388608]{0:T(1024)(128)(4,1)} %bitcast.138), calls=%async_computation.3 | async-start | bytes 8388608
  293.0 35.9 %collective-permute-start.10 = (bf16[4,2,64,1024]{3,2,0,1:T(8,128)(2,1)S(1)}, bf16[4,2,64,1024]{3,2,0,1:T(8,128)(2,1)S(1)}, u32[]{:S(2)}, u32[]{:S(2)}) collective-permute-start(bf16[4,2,64,1024]{3,2,0,1:T(8,128)(2,1)S(1)} %slice_bitcast_fusion.6), channel_id=1, source_target_pairs={{0,4},{1,5},{2,6},{3,7},{4,0},{5,1},{6,2},{7,3},{8,12},{9,13},{10,... | collective-permute-start | bytes 3145736 | tf_op jit(solution)/shard_map/ppermute | solution.py:165
  305.4 34.7 %collective-permute-start.2 = (bf16[4,64,1024]{2,1,0:T(8,128)(2,1)S(1)}, bf16[4,64,1024]{2,1,0:T(8,128)(2,1)S(1)}, u32[]{:S(2)}, u32[]{:S(2)}) collective-permute-start(bf16[4,64,1024]{2,1,0:T(8,128)(2,1)S(1)} %fusion.49), channel_id=1, source_target_pairs={{0,4},{1,5},{2,6},{3,7},{4,0},{5,1},{6,2},{7,3},{8,12},{9,13},{10,... | collective-permute-start | bytes 1572872 | tf_op jit(solution)/shard_map/ppermute | solution.py:165
  309.0 31.3 %collective-permute-start.4 = (bf16[4,64,1024]{2,1,0:T(8,128)(2,1)S(1)}, bf16[4,64,1024]{2,1,0:T(8,128)(2,1)S(1)}, u32[]{:S(2)}, u32[]{:S(2)}) collective-permute-start(bf16[4,64,1024]{2,1,0:T(8,128)(2,1)S(1)} %fusion.50), channel_id=1, source_target_pairs={{0,2},{1,3},{2,0},{3,1},{4,6},{5,7},{6,4},{7,5},{8,10},{9,11},{10,... | collective-permute-start | bytes 1572872 | tf_op jit(solution)/shard_map/ppermute | solution.py:165
  326.3 23.2 %collective-permute-start.9 = (bf16[4,64,1024]{2,1,0:T(8,128)(2,1)S(1)}, bf16[4,64,1024]{2,1,0:T(8,128)(2,1)S(1)}, u32[]{:S(2)}, u32[]{:S(2)}) collective-permute-start(bf16[4,64,1024]{2,1,0:T(8,128)(2,1)S(1)} %fusion.52), channel_id=1, source_target_pairs={{0,4},{1,5},{2,6},{3,7},{4,0},{5,1},{6,2},{7,3},{8,12},{9,13},{10,... | collective-permute-start | bytes 1572872 | tf_op jit(solution)/shard_map/ppermute | solution.py:165
  329.4 20.3 %collective-permute-start.11 = (bf16[4,64,1024]{2,1,0:T(8,128)(2,1)S(1)}, bf16[4,64,1024]{2,1,0:T(8,128)(2,1)S(1)}, u32[]{:S(2)}, u32[]{:S(2)}) collective-permute-start(bf16[4,64,1024]{2,1,0:T(8,128)(2,1)S(1)} %fusion.53), channel_id=1, source_target_pairs={{0,2},{1,3},{2,0},{3,1},{4,6},{5,7},{6,4},{7,5},{8,10},{9,11},{10,... | collective-permute-start | bytes 1572872 | tf_op jit(solution)/shard_map/ppermute | solution.py:165
  340.8 34.7 %collective-permute-start.5 = (bf16[2,64,2048]{2,1,0:T(8,128)(2,1)S(1)}, bf16[2,64,2048]{2,1,0:T(8,128)(2,1)S(1)}, u32[]{:S(2)}, u32[]{:S(2)}) collective-permute-start(bf16[2,64,2048]{2,1,0:T(8,128)(2,1)S(1)} %fusion.51), channel_id=1, source_target_pairs={{0,16},{8,24},{16,0},{24,8},{1,17},{9,25},{17,1},{25,9},{2,18},{10... | collective-permute-start | bytes 1572872 | tf_op jit(solution)/shard_map/ppermute | solution.py:165
  350.2 35.6 %collective-permute-start.12 = (bf16[2,64,2048]{2,1,0:T(8,128)(2,1)S(1)}, bf16[2,64,2048]{2,1,0:T(8,128)(2,1)S(1)}, u32[]{:S(2)}, u32[]{:S(2)}) collective-permute-start(bf16[2,64,2048]{2,1,0:T(8,128)(2,1)S(1)} %fusion.54), channel_id=1, source_target_pairs={{0,16},{8,24},{16,0},{24,8},{1,17},{9,25},{17,1},{25,9},{2,18},{10... | collective-permute-start | bytes 1572872 | tf_op jit(solution)/shard_map/ppermute | solution.py:165
  375.8 15.6 %collective-permute-start.6 = (bf16[64,2048]{1,0:T(8,128)(2,1)S(1)}, bf16[64,2048]{1,0:T(8,128)(2,1)S(1)}, u32[]{:S(2)}, u32[]{:S(2)}) collective-permute-start(bf16[64,2048]{1,0:T(8,128)(2,1)S(1)} %fusion.65), channel_id=1, source_target_pairs={{0,8},{8,0},{16,24},{24,16},{1,9},{9,1},{17,25},{25,17},{2,10},{10... | collective-permute-start | bytes 786440 | tf_op jit(solution)/shard_map/ppermute | solution.py:165
  385.9 11.0 %copy-start.5 = (bf16[128,2048]{1,0:T(8,128)(2,1)S(1)}, bf16[128,2048]{1,0:T(8,128)(2,1)}, u32[]{:S(2)}) copy-start(bf16[128,2048]{1,0:T(8,128)(2,1)} %param.9) | copy-start | bytes 1572868
  385.9 11.4 %copy-start.14 = (bf16[2048,512]{1,0:T(8,128)(2,1)S(1)}, bf16[2048,512]{1,0:T(8,128)(2,1)}, u32[]{:S(2)}) copy-start(bf16[2048,512]{1,0:T(8,128)(2,1)} %param.17) | copy-start | bytes 6291460
  386.0 11.4 %copy-start.15 = (f32[2048]{0:T(1024)S(1)}, f32[2048]{0:T(1024)}, u32[]{:S(2)}) copy-start(f32[2048]{0:T(1024)} %param.16) | copy-start | bytes 24580
  386.1 10.8 %collective-permute-start.13 = (bf16[64,2048]{1,0:T(8,128)(2,1)S(1)}, bf16[64,2048]{1,0:T(8,128)(2,1)S(1)}, u32[]{:S(2)}, u32[]{:S(2)}) collective-permute-start(bf16[64,2048]{1,0:T(8,128)(2,1)S(1)} %fusion.66), channel_id=1, source_target_pairs={{0,8},{8,0},{16,24},{24,16},{1,9},{9,1},{17,25},{25,17},{2,10},{10... | collective-permute-start | bytes 786440 | tf_op jit(solution)/shard_map/ppermute | solution.py:165
  391.4 7.1 %copy-start.1 = (bf16[1,1,704,2048]{3,2,1,0:T(8,128)(2,1)S(1)}, bf16[1,1,704,2048]{3,2,1,0:T(8,128)(2,1)}, u32[]{:S(2)}) copy-start(bf16[1,1,704,2048]{3,2,1,0:T(8,128)(2,1)} %param.15) | copy-start | bytes 8650756
  397.3 1.2 copy-start.9
Sparse Core Ops, SparseCore 0:
  12.9 82.2 all-gather.2
  98.6 78.2 all-gather.4
